TPU v7x, 32 devices: a whole 2x2x4 slice. The times are simulated.
32 devices in a mesh: dp: 16 (over z, y, x), fsdp: 2 (over core).
Axes of the slice: x: 2, y: 2, z: 4, core: 2. Of those that a mesh axis runs over, the one named last changes fastest.
Arguments:
- tokens: bfloat16 [32768, 1024], P(('dp', 'fsdp')), may hold values from -6 to 6
- cotangent: bfloat16 [32768, 1024], P(('dp', 'fsdp')), may hold values from -6 to 6
- lengths: int32 [2], replicated, may hold values from 2048 to 16384, as said below
- norm_gain: bfloat16 [1024], P(('dp', 'fsdp')), may hold values from 0.5 to 1.5
- norm_bias: bfloat16 [1024], P(('dp', 'fsdp')), may hold values from -1.25 to 1.25
- w_one: bfloat16 [1024, 3072], P(('dp', 'fsdp')), may hold values from -0.1875 to 0.1875
- b_one: bfloat16 [3072], P(('dp', 'fsdp')), may hold values from -1.25 to 1.25
- w_two: bfloat16 [1024, 512], P(('dp', 'fsdp')), may hold values from -0.1875 to 0.1875
- b_two: bfloat16 [512], P(('dp', 'fsdp')), may hold values from -1.25 to 1.25
- w_three: bfloat16 [512, 3072], P(('dp', 'fsdp')), may hold values from -0.25 to 0.25
- b_three: bfloat16 [3072], P(('dp', 'fsdp')), may hold values from -1.25 to 1.25
- w_four: bfloat16 [3072, 1024], P(('dp', 'fsdp')), may hold values from -0.109375 to 0.109375
- b_four: bfloat16 [1024], P(('dp', 'fsdp')), may hold values from -1.25 to 1.25
- log_rate: float32 [512, 512], P(('dp', 'fsdp')), may hold values from -9 to -3
- ssm_coeff: float32 [512, 512], P(('dp', 'fsdp')), may hold values from -0.009765625 to 0.009765625
- ssm_skip: float32 [512], P(('dp', 'fsdp')), may hold values from 0.5 to 1.5
Outputs:
- mixed: bfloat16 [32768, 1024], P(('dp', 'fsdp'))
- input_grad: bfloat16 [32768, 1024], P(('dp', 'fsdp'))
- grad_norm_gain: float32 [1024], P(('dp', 'fsdp'))
- grad_norm_bias: float32 [1024], P(('dp', 'fsdp'))
- grad_w_one: float32 [1024, 3072], P(('dp', 'fsdp'))
- grad_b_one: float32 [3072], P(('dp', 'fsdp'))
- grad_w_two: float32 [1024, 512], P(('dp', 'fsdp'))
- grad_b_two: float32 [512], P(('dp', 'fsdp'))
- grad_w_three: float32 [512, 3072], P(('dp', 'fsdp'))
- grad_b_three: float32 [3072], P(('dp', 'fsdp'))
- grad_w_four: float32 [3072, 1024], P(('dp', 'fsdp'))
- grad_b_four: float32 [1024], P(('dp', 'fsdp'))
- grad_log_rate: float32 [512, 512], P(('dp', 'fsdp'))
- grad_ssm_coeff: float32 [512, 512], P(('dp', 'fsdp'))
- grad_ssm_skip: float32 [512], P(('dp', 'fsdp'))
Inputs may be any that keep to these rules, and one draw needn't show every extreme that they name: `lengths`: every bucket's length is at least 2048; one bucket in every draw holds a full sequence of 16384 tokens.
All inputs are finite; a program needn't handle non-finite values.
Results may differ from a plain program's by a relative error of at most 0.0071.
Values may be sent and summed in bfloat16 or wider, within the bound.
No kernel may reach another device: no remote copies, remote signals or barrier semaphores. Data moves between devices by JAX's collectives and lax.ppermute only.
A program may use at most 192 MiB of HBM per device.

v0:
```python
import functools

import jax
import jax.numpy as jnp
from jax import lax
from jax.experimental import pallas as pl
from jax.experimental.pallas import tpu as pltpu
from jax.sharding import PartitionSpec as P

SEQ = 16384
QBLK = 256
F32 = jnp.float32
BF = jnp.bfloat16
SWAP = [(0, 1), (1, 0)]
ROOM = 52
TOOK = dict(
    norm=10, mixer_tables=12, mixer_forward=13, early=24, gate=13, grad_four=11, grad_one=12,
    mixer_backward=20, grad_three=8, out=20, tail=1, input_grad=7,
)


def costing(name):
    return pl.CostEstimate(flops=int(TOOK[name] * 3.3e+06 * 300), bytes_accessed=int(TOOK[name] * 3.3e+06), transcendentals=0)


def mm(left, right, left_dim, right_dim):
    return lax.dot_general(
        left, right, (((left_dim,), (right_dim,)), ((), ())), preferred_element_type=F32
    )


def split(value):
    high = value.astype(BF)
    return high, (value - high.astype(F32)).astype(BF)


def iotas(rows, cols):
    return (
        lax.broadcasted_iota(jnp.int32, (rows, cols), 0),
        lax.broadcasted_iota(jnp.int32, (rows, cols), 1),
    )


def shift_rows(x, k, backward):
    n = x.shape[0]
    row = iotas(*x.shape)[0]
    if backward:
        return jnp.where(row < n - k, pltpu.roll(x, n - k, 0), 0.0)
    return jnp.where(row >= k, pltpu.roll(x, k, 0), 0.0)


def states(x, rate, group, backward):
    blocks = x.shape[0] // group
    order = list(range(blocks))[:: -1 if backward else 1]
    decay = jnp.exp(-rate * float(QBLK))
    local, state = {}, None
    for b in order:
        local[b] = state
        here = x[b * group : (b + 1) * group]
        state = here if state is None else state * decay + here
    k = 1
    while k < group:
        state = state + shift_rows(state, k, backward) * jnp.exp(-rate * float(QBLK * blocks * k))
        k *= 2
    carry = shift_rows(state, 1, backward)
    out = {}
    for step, b in enumerate(order):
        far = carry * jnp.exp(-rate * float(QBLK * step)) if step else carry
        out[b] = far if local[b] is None else far + local[b]
    return jnp.concatenate([out[b] for b in range(blocks)], axis=0)


def flip_matrix():
    i, j = iotas(QBLK, QBLK)
    return jnp.where(i + j == QBLK - 1, 1.0, 0.0).astype(BF)


def base_of(rate):
    return jnp.where(rate * float(QBLK) < 1.0, 1.0, 0.0)


def row_sums(x):
    return jnp.sum(x.astype(F32), axis=1, keepdims=True)


def through(rows, table, base):
    return mm(rows, table, 1, 0) + row_sums(rows) * base


def table_kernel(lr_ref, co_ref, d_ref, dt_ref, t_ref):
    i, j = iotas(QBLK, QBLK)
    for c in range(lr_ref.shape[0]):
        rate, coeff = jnp.exp(lr_ref[c]), co_ref[c]
        row = lax.broadcasted_iota(jnp.int32, (8, rate.shape[1]), 0).astype(F32)
        table = jnp.exp(-rate * row)
        step = 8
        while step < QBLK:
            table = jnp.concatenate([table, table * jnp.exp(-rate * float(step))], axis=0)
            step *= 2
        lowered = table - base_of(rate)
        d_ref[c] = lowered.astype(BF)
        turned = lowered.T
        dt_ref[c] = turned.astype(BF)
        high, low = split(jnp.broadcast_to(coeff, (8, coeff.shape[1])))
        t_high, t_low = split(turned)
        kern = (
            mm(high, t_high, 1, 0) + mm(low, t_high, 1, 0) + mm(high, t_low, 1, 0)
        )[0:1] + row_sums(coeff * base_of(rate))
        rolled = pltpu.roll(jnp.broadcast_to(kern, (QBLK, QBLK)), 0, 1, stride=1, stride_axis=0)
        t_ref[c] = jnp.where(j >= i, rolled, 0.0).astype(BF)


def far_rows(entering, scale, turned, base):
    rows = entering.shape[0]
    scaled = entering * scale
    both = mm(jnp.concatenate(split(scaled), axis=0), turned, 1, 0)
    return both[:rows] + both[rows:] + row_sums(scaled * base)


def lanes_of(b, turn, total):
    start = b * QBLK + turn * (total // 2)
    start = jnp.where(start >= total, start - total, start)
    return pl.ds(pl.multiple_of(start, QBLK), QBLK)


def take_rows(x_ref, rows_ref, turn):
    group, _, total = x_ref.shape
    for b in range(0, total // QBLK, 2):
        pair = [
            jnp.swapaxes(x_ref[:, :, lanes_of(b + k, turn, total)].astype(F32), 0, 1)
            for k in range(2)
        ]
        rows_ref[:, b * group : (b + 2) * group, :] = jnp.concatenate(pair, axis=1).astype(BF)


def give_rows(rows_ref, x_ref, turn):
    group, _, total = x_ref.shape
    for b in range(0, total // QBLK, 2):
        pair = rows_ref[:, b * group : (b + 2) * group, :].astype(F32)
        for k in range(2):
            x_ref[:, :, lanes_of(b + k, turn, total)] = jnp.swapaxes(
                pair[:, k * group : (k + 1) * group], 0, 1
            ).astype(BF)


def forward_kernel(turn_ref, v_ref, d_ref, dt_ref, t_ref, lr_ref, co_ref, sk_ref, y_ref, en_ref, rows_ref, back_ref):
    per, group, turn = d_ref.shape[0], v_ref.shape[0], turn_ref[0]
    part, parts = pl.program_id(1), pl.num_programs(1)
    count = rows_ref.shape[1]

    @pl.when(part == 0)
    def _():
        take_rows(v_ref, rows_ref, turn)

    mine = rows_ref[pl.ds(part * per, per)]
    flipped = mm(mine.reshape(per * count, QBLK), flip_matrix(), 1, 0).astype(BF)
    for c in range(per):
        v = mine[c]
        rate = jnp.exp(lr_ref[c])
        base = base_of(rate)
        ends = through(flipped[c * count : (c + 1) * count], d_ref[c], base)
        entering = states(ends, rate, group, False)
        en_ref[c] = entering
        far = far_rows(entering, co_ref[c] * jnp.exp(-rate), dt_ref[c], base)
        back_ref[part * per + c] = (
            far + mm(v, t_ref[c], 1, 0) + sk_ref[c][:, :1] * v.astype(F32)
        ).astype(BF)

    @pl.when(part == parts - 1)
    def _():
        give_rows(back_ref, y_ref, turn)


def backward_kernel(
    turn_ref, v_ref, dy_ref, en_ref, d_ref, dt_ref, t_ref, lr_ref, co_ref, sk_ref,
    dv_ref, gr_ref, gc_ref, gs_ref, v_rows_ref, dy_rows_ref, back_ref,
):
    per, group, turn = d_ref.shape[0], v_ref.shape[0], turn_ref[0]
    part, parts = pl.program_id(1), pl.num_programs(1)
    count = v_rows_ref.shape[1]
    rows = per * count

    @pl.when(part == 0)
    def _():
        take_rows(v_ref, v_rows_ref, turn)
        take_rows(dy_ref, dy_rows_ref, turn)

    flip = flip_matrix()
    v_all = v_rows_ref[pl.ds(part * per, per)].reshape(rows, QBLK)
    dy_all = dy_rows_ref[pl.ds(part * per, per)].reshape(rows, QBLK)
    flipped = mm(jnp.concatenate([v_all, dy_all], axis=0), flip, 1, 0)
    lane = lax.broadcasted_iota(jnp.int32, (rows, QBLK), 1).astype(F32)
    v_lag = (flipped[:rows] * lane).astype(BF)
    dy_lag = (dy_all.astype(F32) * lane).astype(BF)
    flipped = flipped.astype(BF)
    i, j = iotas(QBLK, QBLK)
    lag = lax.broadcasted_iota(jnp.int32, (1, QBLK), 1).astype(F32)
    back = []
    for c in range(per):
        here = slice(c * count, (c + 1) * count)
        dy = dy_all[here]
        v_flip, dy_flip = flipped[here], flipped[rows + c * count : rows + (c + 1) * count]
        rate, coeff = jnp.exp(lr_ref[c]), co_ref[c]
        base = base_of(rate)
        pairs = pltpu.roll(mm(v_flip, dy, 0, 0), 1, 1, stride=1, stride_axis=0)
        near = jnp.sum(jnp.where(j <= i, pairs, 0.0), axis=0, keepdims=True)
        near_rows = jnp.concatenate(
            split(
                jnp.concatenate(
                    [jnp.broadcast_to(near, (8, QBLK)), jnp.broadcast_to(near * lag, (8, QBLK))],
                    axis=0,
                )
            ),
            axis=0,
        )
        sums = through(
            jnp.concatenate([dy, dy_lag[here], v_lag[here], near_rows], axis=0), d_ref[c], base
        )
        starts, starts_lag, ends_lag = (sums[k * count : (k + 1) * count] for k in range(3))
        inner = sums[3 * count : 3 * count + 16] + sums[3 * count + 16 :]
        leaving = states(starts, rate, group, True)
        entering = en_ref[c]
        one = jnp.exp(-rate)
        far = far_rows(leaving, coeff * one, dt_ref[c], base)
        back.append(
            (
                far + mm(dy_flip, t_ref[c], 1, 0) + sk_ref[c][:, :1] * dy_flip.astype(F32)
            ).astype(BF)
        )
        whole = jnp.exp(-rate * float(QBLK))
        outer = jnp.sum(entering * starts, axis=0, keepdims=True)
        moment = jnp.sum(
            ends_lag * leaving + entering * (starts_lag + (float(QBLK) * whole) * leaving),
            axis=0,
            keepdims=True,
        )
        gc_ref[c] = inner[0:1] + one * outer
        gr_ref[c] = -(coeff * rate) * (inner[8:9] + one * (moment + outer))
        gs_ref[c] = jnp.broadcast_to(near[:, :1], (1, 128))
    turned = mm(jnp.concatenate(back, axis=0), flip, 1, 0).astype(BF)
    back_ref[pl.ds(part * per, per)] = turned.reshape(per, count, QBLK)

    @pl.when(part == parts - 1)
    def _():
        give_rows(back_ref, dv_ref, turn)


def mixer_tables(log_rate, coeff):
    chans, _, n = log_rate.shape
    per = 4

    def spec(rows, cols):
        return pl.BlockSpec((per, rows, cols), lambda i: (i, 0, 0))

    shapes = [(QBLK, n), (n, QBLK), (QBLK, QBLK)]
    return pl.pallas_call(
        table_kernel,
        grid=(chans // per,),
        in_specs=[spec(1, n)] * 2,
        out_specs=[spec(*shape) for shape in shapes],
        out_shape=[jax.ShapeDtypeStruct((chans,) + shape, BF) for shape in shapes],
        compiler_params=pltpu.CompilerParams(vmem_limit_bytes=ROOM * 2**20),
        cost_estimate=costing("mixer_tables"),
        name="mixer_tables",
    )(log_rate, coeff)


def mixer_call(kernel, turn, tokens_in, by_channel, outs, name):
    group, chans, total = tokens_in[0].shape
    tall, per = 16, 8
    parts = tall // per
    count = group * (total // QBLK)

    def spec(shape):
        return pl.BlockSpec((per,) + tuple(shape[1:]), lambda i, j, *_: (i * parts + j, 0, 0))

    wide = pl.BlockSpec((group, tall, total), lambda i, j, *_: (0, i, 0))
    return pl.pallas_call(
        kernel,
        grid_spec=pltpu.PrefetchScalarGridSpec(
            num_scalar_prefetch=1,
            grid=(chans // tall, parts),
            in_specs=[wide] * len(tokens_in) + [spec(x.shape) for x in by_channel],
            out_specs=[wide] + [spec(shape) for shape, _ in outs],
            scratch_shapes=[pltpu.VMEM((tall, count, QBLK), BF)] * (len(tokens_in) + 1),
        ),
        out_shape=[jax.ShapeDtypeStruct((group, chans, total), BF)]
        + [jax.ShapeDtypeStruct(shape, kind) for shape, kind in outs],
        compiler_params=pltpu.CompilerParams(vmem_limit_bytes=ROOM * 2**20),
        cost_estimate=costing(name),
        name=name,
    )(turn, *tokens_in, *by_channel)


def mixer_forward(turn, v, tables, params):
    group, chans, total = v.shape
    n = params[0].shape[2]
    states_of = (chans, group * (total // QBLK), n)
    return mixer_call(
        forward_kernel, turn, [v], [*tables, *params], [(states_of, F32)], "mixer_forward"
    )


def mixer_backward(turn, v, dy, entering, tables, params):
    chans, n = v.shape[1], params[0].shape[2]
    return mixer_call(
        backward_kernel,
        turn,
        [v, dy],
        [entering, *tables, *params],
        [((chans, 1, n), F32), ((chans, 1, n), F32), ((chans, 1, 128), F32)],
        "mixer_backward",
    )


TILE = 512


def call(kernel, grid, core, ins, outs, name, room, scratch=()):
    return pl.pallas_call(
        kernel,
        grid_spec=pltpu.PrefetchScalarGridSpec(
            num_scalar_prefetch=1,
            grid=(grid,),
            in_specs=[
                pl.BlockSpec(block, index, pipeline_mode=None if index in MOVING else pl.Buffered(1))
                for _, block, index in ins
            ],
            out_specs=[pl.BlockSpec(block, index) for _, _, block, index in outs],
            scratch_shapes=list(scratch),
        ),
        out_shape=[jax.ShapeDtypeStruct(shape, kind) for shape, kind, _, _ in outs],
        compiler_params=pltpu.CompilerParams(vmem_limit_bytes=room * 2**20),
        cost_estimate=costing(name),
        name=name,
    )(core, *[array for array, _, _ in ins])


def row_tile(m, _):
    return (m, 0)


def col_tile(m, _):
    return (0, m)


def turned_tile(m, _):
    half = pl.num_programs(0) // 2
    return (0, jnp.where(m < half, m + half, m - half))


def fixed(m, _):
    return (0, 0)


MOVING = (row_tile, col_tile, turned_tile)


def first_rows(m, _):
    return (jnp.minimum(m, pl.num_programs(0) // 2 - 1), 0)


def last_rows(m, _):
    return (jnp.maximum(m - pl.num_programs(0) // 2, 0), 0)


def strips_of(start, stop, strip):
    while start < stop:
        k = start // strip
        end = min(stop, (k + 1) * strip)
        yield k, slice(start - k * strip, end - k * strip)
        start = end


def strip_columns(ref, total, start, stop, order):
    rows = ref.shape[2] // (total // ref.shape[3])
    return jnp.concatenate(
        [
            jnp.concatenate(
                [
                    ref[chip, core, k * rows : (k + 1) * rows, lanes]
                    for chip in order
                    for core in range(ref.shape[1])
                ],
                axis=0,
            )
            for k, lanes in strips_of(start, stop, ref.shape[3])
        ],
        axis=1,
    )


def strip_rows(ref, strips, start, stop):
    rows = ref.shape[2] // strips
    return jnp.concatenate(
        [
            jnp.concatenate(
                [
                    ref[chip, 0, k * rows + part.start : k * rows + part.stop, :]
                    for chip, part in strips_of(start, stop, rows)
                ],
                axis=0,
            )
            for k in range(strips)
        ],
        axis=1,
    )


def col_sum(x):
    return jnp.sum(x.astype(F32), axis=0, keepdims=True)


def hat_of(x):
    x = x.astype(F32)
    centered = x - jnp.mean(x, axis=-1, keepdims=True)
    inv_std = lax.rsqrt(jnp.mean(centered * centered, axis=-1, keepdims=True) + 1e-05)
    return centered * inv_std, inv_std


def slope_and_gelu(h):
    phi = 0.5 + 0.5 * lax.erf(h * 0.7071067811865476)
    return h * phi, phi + h * jnp.exp(-0.5 * h * h) * 0.3989422804014327


def norm_kernel(
    _, tok_ref, cot_ref, live_ref, gain_ref, bias_ref, w_ref, b_ref, n_ref, g_ref, v_ref, s_ref, sum_ref
):
    m = pl.program_id(0)

    @pl.when(m == 0)
    def _():
        sum_ref[...] = jnp.zeros_like(sum_ref)

    hat, _ = hat_of(tok_ref[...])
    normed = (hat * gain_ref[...] + bias_ref[...]).astype(BF)
    n_ref[...] = normed
    g = jnp.where(live_ref[...][:, :1] > 0.0, cot_ref[...], jnp.zeros((), BF))
    g_ref[...] = g

    @pl.when(m < pl.num_programs(0) // 2)
    def _():
        sum_ref[...] += col_sum(g)

    v, s = slope_and_gelu(mm(w_ref[...], normed, 1, 1) + b_ref[...][:, :1])
    v_ref[...] = v.astype(BF)
    s_ref[...] = s.astype(BF)


def norm_call(core, tok, cot, live, gain, bias, w_turned, b):
    tokens, width = tok.shape
    chans = w_turned.shape[0]
    rows, cols = (TILE, width), (chans, TILE)
    return call(
        norm_kernel,
        tokens // TILE,
        core,
        [
            (tok, rows, row_tile),
            (cot, rows, row_tile),
            (live, (TILE, 128), row_tile),
            (gain, (1, width), fixed),
            (bias, (1, width), fixed),
            (w_turned, (chans, width), fixed),
            (b, (chans, 128), fixed),
        ],
        [((tokens, width), BF, rows, row_tile)] * 2
        + [((chans, tokens), BF, cols, col_tile)] * 2
        + [((1, width), F32, (1, width), fixed)],
        "norm",
        ROOM,
    )


def early_kernel(
    _, x_ref, g_ref, b1_ref, w1_ref, w4_ref, w3m_ref, w3o_ref,
    u_ref, dzs_ref, dgate_ref, mine_ref, other_ref, sum_ref, *, order,
):
    total = u_ref.shape[1]
    cols, chips = 768, range(w1_ref.shape[0])
    e_strips = g_ref.shape[1] // w4_ref.shape[3]

    @pl.when(pl.program_id(0) == 0)
    def _():
        sum_ref[...] = jnp.zeros_like(sum_ref)

    for n in range(total // cols):
        at = slice(n * cols, (n + 1) * cols)
        w1 = strip_columns(w1_ref, total, at.start, at.stop, chips)
        u, s = slope_and_gelu(mm(x_ref[...], w1, 1, 0) + b1_ref[:, at])
        dz = mm(g_ref[...], strip_rows(w4_ref, e_strips, at.start, at.stop), 1, 1)
        dgate = (dz * u).astype(BF)
        u_ref[:, at] = u.astype(BF)
        dzs_ref[:, at] = (dz * s).astype(BF)
        dgate_ref[:, at] = dgate
        sum_ref[:, at] += col_sum(dgate)
    mine_ref[...] = mm(strip_columns(w3m_ref, total, 0, total, order), dgate_ref[...], 1, 1)
    other = mm(strip_columns(w3o_ref, total, 0, total, order), dgate_ref[...], 1, 1)
    other_ref[...] = other.astype(BF)


def early_call(core, x, g, b1, weights, order):
    tokens, width = x.shape
    cols = b1.shape[1]
    chans = weights[2][1][2] * weights[2][1][3] * len(order) // cols
    wide, tall = (TILE, cols), (chans, TILE)
    return call(
        functools.partial(early_kernel, order=order),
        tokens // TILE,
        core,
        [
            (x, (TILE, width), row_tile),
            (g, (TILE, width), row_tile),
            (b1, (1, cols), fixed),
            *weights,
        ],
        [((tokens, cols), BF, wide, row_tile)] * 3
        + [
            ((chans, tokens), F32, tall, col_tile),
            ((chans, tokens), BF, tall, turned_tile),
            ((1, cols), F32, (1, cols), fixed),
        ],
        "early",
        ROOM,
    )


def gate_kernel(
    _, ym_ref, yo_ref, b3_ref, u_ref, dzs_ref, w3m_ref, w3o_ref, z_ref, dh_ref, sum_ref, *, order
):
    total, cols = u_ref.shape[1], 256

    @pl.when(pl.program_id(0) == 0)
    def _():
        sum_ref[...] = jnp.zeros_like(sum_ref)

    y = jnp.concatenate([ym_ref[...], yo_ref[...]], axis=0).T
    for n in range(total // cols):
        at = slice(n * cols, (n + 1) * cols)
        w3 = jnp.concatenate(
            [strip_columns(ref, total, at.start, at.stop, order) for ref in (w3m_ref, w3o_ref)],
            axis=0,
        )
        gate = mm(y, w3, 1, 0) + b3_ref[:, at]
        z_ref[:, at] = (u_ref[:, at].astype(F32) * gate).astype(BF)
        dh = (dzs_ref[:, at].astype(F32) * gate).astype(BF)
        dh_ref[:, at] = dh
        sum_ref[:, at] += col_sum(dh)


def gate_call(core, y_mine, y_other, b3, u, dzs, weights, order):
    tokens, cols = u.shape
    wide, tall = (TILE, cols), (y_mine.shape[0], TILE)
    return call(
        functools.partial(gate_kernel, order=order),
        tokens // TILE,
        core,
        [
            (y_mine, tall, col_tile),
            (y_other, tall, turned_tile),
            (b3, (1, cols), fixed),
            (u, wide, row_tile),
            (dzs, wide, row_tile),
            *weights[2:],
        ],
        [
            ((tokens, cols), BF, wide, row_tile),
            ((tokens, cols), BF, wide, row_tile),
            ((1, cols), F32, (1, cols), fixed),
        ],
        "gate",
        ROOM,
    )


def out_kernel(_, z_ref, dh_ref, w1_ref, w4_ref, om_ref, oo_ref, p_ref):
    m, total = pl.program_id(0), z_ref.shape[1]
    chips = range(w1_ref.shape[0])
    e_strips = om_ref.shape[1] // w4_ref.shape[3]
    p_ref[...] = mm(dh_ref[...], strip_columns(w1_ref, total, 0, total, chips), 1, 1).astype(BF)
    out = mm(z_ref[...], strip_rows(w4_ref, e_strips, 0, total), 1, 0)

    @pl.when(m < pl.num_programs(0) // 2)
    def _():
        om_ref[...] = out

    @pl.when(m >= pl.num_programs(0) // 2)
    def _():
        oo_ref[...] = out.astype(BF)


def out_call(core, z, dh, width, weights):
    tokens, cols = z.shape
    wide, rows = (TILE, cols), (TILE, width)
    return call(
        out_kernel,
        tokens // TILE,
        core,
        [(z, wide, row_tile), (dh, wide, row_tile), *weights[:2]],
        [
            ((tokens // 2, width), F32, rows, first_rows),
            ((tokens // 2, width), BF, rows, last_rows),
            ((tokens, width), BF, rows, row_tile),
        ],
        "out",
        ROOM,
    )


def tail_kernel(
    _, dv_ref, s_ref, w_ref, p_ref, tok_ref, n_ref, grad_ref, pm_ref, po_ref, gain_ref, bias_ref, sum_ref, total_ref
):
    m = pl.program_id(0)

    @pl.when(m == 0)
    def _():
        gain_ref[...] = jnp.zeros_like(gain_ref)
        bias_ref[...] = jnp.zeros_like(bias_ref)
        sum_ref[...] = jnp.zeros_like(sum_ref)
        total_ref[...] = jnp.zeros_like(total_ref)

    dh = (dv_ref[...].astype(F32) * s_ref[...].astype(F32)).astype(BF)
    total_ref[...] += mm(dh, n_ref[...], 1, 0)
    for k in range(dh.shape[1] // 128):
        sum_ref[...] += dh[:, k * 128 : (k + 1) * 128].astype(F32)
    p = p_ref[...].astype(F32) + mm(dh.T, w_ref[...], 1, 0)
    hat, _ = hat_of(tok_ref[...])
    gain_ref[...] += col_sum(p * hat)
    bias_ref[...] += col_sum(p)

    @pl.when(m == pl.num_programs(0) - 1)
    def _():
        grad_ref[...] = total_ref[...].T.astype(BF)

    @pl.when(m < pl.num_programs(0) // 2)
    def _():
        pm_ref[...] = p

    @pl.when(m >= pl.num_programs(0) // 2)
    def _():
        po_ref[...] = p.astype(BF)


def tail_call(core, dv, slope, w_turned, p, tok, normed):
    chans, tokens = dv.shape
    width = p.shape[1]
    rows, cols = (TILE, width), (chans, TILE)
    return call(
        tail_kernel,
        tokens // TILE,
        core,
        [
            (dv, cols, col_tile),
            (slope, cols, col_tile),
            (w_turned, (chans, width), fixed),
            (p, rows, row_tile),
            (tok, rows, row_tile),
            (normed, rows, row_tile),
        ],
        [
            ((width, chans), BF, (width, chans), fixed),
            ((tokens // 2, width), F32, rows, first_rows),
            ((tokens // 2, width), BF, rows, last_rows),
            ((1, width), F32, (1, width), fixed),
            ((1, width), F32, (1, width), fixed),
            ((chans, 128), F32, (chans, 128), fixed),
        ],
        "tail",
        ROOM,
        [pltpu.VMEM((chans, width), F32)],
    )


def input_kernel(_, mine_ref, got_ref, tok_ref, g_ref, gain_ref, out_ref):
    hat, inv_std = hat_of(tok_ref[...])
    grad = (mine_ref[...] + got_ref[...].astype(F32)) * gain_ref[...]
    out_ref[...] = (
        g_ref[...].astype(F32)
        + inv_std
        * (
            grad
            - jnp.mean(grad, axis=-1, keepdims=True)
            - hat * jnp.mean(grad * hat, axis=-1, keepdims=True)
        )
    ).astype(BF)


def input_call(core, mine, got, tok, g, gain):
    tokens, width = mine.shape
    rows = (256, width)
    return call(
        input_kernel,
        tokens // 256,
        core,
        [(x, rows, row_tile) for x in (mine, got, tok, g)] + [(gain, (1, width), fixed)],
        [((tokens, width), BF, rows, row_tile)],
        "input_grad",
        ROOM,
    )[0]

def keep_and_send(here, out_ref, runs, keep_ref, send_refs):
    for k, ref in enumerate((keep_ref, *send_refs)):
        part = jnp.concatenate(
            [
                out_ref[pl.ds(pl.multiple_of((at + (here ^ k)) * runs, runs), runs), :]
                for at in range(0, out_ref.shape[0] // runs, 4)
            ],
            axis=0,
        )
        ref[...] = part.astype(ref.dtype)


def grad_kernel(here_ref, a_ref, b_ref, keep_ref, s1_ref, s2_ref, s3_ref, out_ref, *, runs):
    out_ref[...] = mm(a_ref[...], b_ref[...], 0, 0)
    keep_and_send(here_ref[0], out_ref, runs, keep_ref, (s1_ref, s2_ref, s3_ref))


def grad_call(here, a, b, runs, tile, name):
    rows, cols = a.shape[1], b.shape[1]
    part, shape = (tile // 4, cols), (rows // 4, cols)
    return call(
        functools.partial(grad_kernel, runs=runs),
        rows // tile,
        here,
        [(a, (a.shape[0], tile), col_tile), (b, b.shape, fixed)],
        [(shape, kind, part, row_tile) for kind in (F32, BF, BF, BF)],
        name,
        ROOM,
        [pltpu.VMEM((tile, cols), F32)],
    )


def mixed_grad_kernel(here_ref, ym_ref, yo_ref, b_ref, keep_ref, s1_ref, s2_ref, s3_ref, out_ref, *, runs):
    half, rows = b_ref.shape[0] // 2, ym_ref.shape[0]
    out_ref[:rows] = mm(ym_ref[...], b_ref[...], 1, 0)
    out_ref[rows:] = mm(yo_ref[:, half:], b_ref[:half], 1, 0) + mm(
        yo_ref[:, :half], b_ref[half:], 1, 0
    )
    keep_and_send(here_ref[0], out_ref, runs, keep_ref, (s1_ref, s2_ref, s3_ref))


def mixed_grad_call(here, y_mine, y_other, b, runs, name):
    rows, cols, tile = 2 * y_mine.shape[0], b.shape[1], 512
    part, shape = (rows // 4, tile), (rows // 4, cols)
    return call(
        functools.partial(mixed_grad_kernel, runs=runs),
        cols // tile,
        here,
        [(y_mine, y_mine.shape, fixed), (y_other, y_other.shape, fixed), (b, (b.shape[0], tile), col_tile)],
        [(shape, kind, part, col_tile) for kind in (F32, BF, BF, BF)],
        name,
        ROOM,
        [pltpu.VMEM((rows, tile), F32)],
    )


def after(x, *others):
    return lax.optimization_barrier((x,) + others)[0]


def swap_cores(x):
    return lax.ppermute(x, "fsdp", SWAP)


def across(x, size, flip):
    return lax.ppermute(x, "dp", [(i, i ^ flip) for i in range(size)])


def bit_of(bit):
    return (lax.axis_index("dp") >> bit) & 1


def gather_bits(x, size, order, layout):
    have = []
    for bit in order:
        other = across(x, size, 1 << bit)
        mine = bit_of(bit) == 1
        have = [b for b in layout if b in have or b == bit]
        x = jnp.stack(
            [jnp.where(mine, other, x), jnp.where(mine, x, other)], axis=have.index(bit)
        )
    return x


def scatter_bits(x, size, order, layout, send_type):
    have = list(layout)
    for bit in order:
        axis = have.index(bit)
        mine = bit_of(bit)
        theirs = lax.dynamic_index_in_dim(x, 1 - mine, axis, keepdims=False)
        kept = lax.dynamic_index_in_dim(x, mine, axis, keepdims=False)
        x = kept.astype(F32) + across(theirs.astype(send_type), size, 1 << bit).astype(F32)
        have.remove(bit)
    return x


def per_device(
    size,
    tokens,
    cotangent,
    lengths,
    norm_gain,
    norm_bias,
    w_one,
    b_one,
    w_two,
    b_two,
    w_three,
    b_three,
    w_four,
    b_four,
    log_rate,
    ssm_coeff,
    ssm_skip,
):
    bits = size.bit_length() - 1
    tok_dev, width = tokens.shape
    rows_e, rows_f, rows_h = w_one.shape[0], w_four.shape[0], w_three.shape[0]
    f_half, h_half = size * rows_f, size * rows_h
    buckets = lengths.shape[0]
    group = size // buckets
    group_bits = group.bit_length() - 1
    chans = buckets * rows_h
    tok_chip = 2 * tok_dev
    per_dev = tok_dev // QBLK
    nstate = log_rate.shape[1]
    natural = list(range(bits))[::-1]
    by_owner = natural[bits - group_bits :] + natural[: bits - group_bits]
    top = natural[: bits - group_bits]
    order_a = list(range(2, bits)) + [0, 1]
    order_b = list(range(2, bits)) + [1, 0]
    core = lax.axis_index("fsdp")
    first = core == 0
    chip = lax.axis_index("dp")
    core_at = jnp.reshape(core, (1,)).astype(jnp.int32)
    everyone = ("dp", "fsdp")

    def natural_pair(mine, other, axis=0):
        return jnp.stack(
            [jnp.where(first, mine, other), jnp.where(first, other, mine)], axis=axis
        )

    def mine_other(parts, axis):
        a = lax.index_in_dim(parts, 0, axis, keepdims=False)
        b = lax.index_in_dim(parts, 1, axis, keepdims=False)
        return jnp.where(first, a, b), jnp.where(first, b, a)

    tok_pair = jnp.concatenate([tokens, swap_cores(tokens)], axis=0)
    cot_pair = jnp.concatenate([cotangent, swap_cores(cotangent)], axis=0)

    two_parts = jnp.moveaxis(
        w_two.reshape(rows_e, buckets, group, 2, rows_h), (3, 2, 1), (0, 2, 3)
    ).reshape(2, rows_e, h_half)
    vec = jnp.concatenate([norm_gain, norm_bias, b_four, b_one, b_three, b_two])
    vec_len = vec.shape[0]
    vec_rows = -(-vec_len // h_half)
    vec = jnp.pad(vec, (0, vec_rows * h_half - vec_len)).reshape(1, vec_rows, h_half)
    small = jnp.concatenate(
        [two_parts, jnp.broadcast_to(vec, (2, vec_rows, h_half))], axis=1
    )
    small = jnp.broadcast_to(small[None], (size, 2) + small.shape[1:])
    small = lax.all_to_all(
        small.reshape((2 * size,) + small.shape[2:]), everyone, split_axis=0, concat_axis=0
    )
    two_turned = small[:, :rows_e].reshape(width, h_half).T
    vecs = small[:, rows_e:].reshape(2 * size, -1)[:, :vec_len].astype(F32)
    gain_f = vecs[:, :rows_e].reshape(1, width)
    nbias_f = vecs[:, rows_e : 2 * rows_e].reshape(1, width)
    bfour_f = vecs[:, 2 * rows_e : 3 * rows_e].reshape(1, width)
    own_vecs, _ = mine_other(vecs.reshape(size, 2, vec_len)[:, :, 3 * rows_e :], 1)
    bone_f = own_vecs[:, :rows_f].reshape(1, f_half)
    bthree_f = own_vecs[:, rows_f : 2 * rows_f].reshape(1, f_half)
    btwo_f = (
        own_vecs[:, 2 * rows_f :].reshape(buckets, group, rows_h).swapaxes(0, 1).reshape(h_half, 1)
    )

    strip = 512
    f_strips, e_strips = f_half // strip, width // strip

    def by_half(x):
        rows = x.shape[0]
        parts = jnp.moveaxis(x.reshape(rows, size, 2, rows_f), 2, 0).reshape(2, rows, f_half)
        parts = jnp.moveaxis(parts.reshape(2, rows, f_strips, strip), 2, 1)
        return parts.reshape(2 * f_strips * rows, strip)

    packed = jnp.concatenate(
        [w_four[:, k * strip : (k + 1) * strip] for k in range(e_strips)]
        + [by_half(w_one), by_half(w_three)],
        axis=0,
    )
    gathered = lax.all_gather(packed, everyone, axis=0)
    four_end = e_strips * rows_f
    one_end = four_end + 2 * f_strips * rows_e
    gathered = gathered.reshape(size, 2, -1, strip)
    one_rows, three_rows = f_strips * rows_e, f_strips * rows_h

    def block(chips, cores, rows):
        return (chips, cores, rows, strip)

    if rows_h % 16 == 0 and four_end % one_rows == 0 and one_end % three_rows == 0:
        one_at, three_at = four_end // one_rows, one_end // three_rows
        order = [b * group + j for j in range(group) for b in range(buckets)]
        weights = [
            (gathered, block(size, 2, one_rows), lambda m, c: (0, 0, one_at + c[0], 0)),
            (gathered, block(size, 1, four_end), lambda m, c: (0, c[0], 0, 0)),
            (gathered, block(size, 1, three_rows), lambda m, c: (0, c[0], three_at + c[0], 0)),
            (gathered, block(size, 1, three_rows), lambda m, c: (0, 1 - c[0], three_at + c[0], 0)),
        ]
    else:
        order = [0]
        four_half = gathered[:, :, :four_end].reshape(size, 2, e_strips, rows_f, strip)
        four_half = lax.dynamic_index_in_dim(four_half, core, 1, keepdims=False).swapaxes(0, 1)
        one_half = gathered[:, :, four_end:one_end].reshape(2 * size, 2, f_strips, rows_e, strip)
        one_half = lax.dynamic_index_in_dim(one_half, core, 1, keepdims=False).swapaxes(0, 1)
        three_half = gathered[:, :, one_end:].reshape(
            buckets, group, 2, 2, f_strips, rows_h, strip
        )
        three_half = lax.dynamic_index_in_dim(three_half, core, 3, keepdims=False)
        three_half = jnp.transpose(three_half, (2, 3, 1, 0, 4, 5))
        three_half = mine_other(three_half, 0)
        weights = [
            (x.reshape(1, 1, -1, strip), block(1, 1, x.size // strip), lambda m, c: (0, 0, 0, 0))
            for x in (one_half, four_half, *three_half)
        ]

    params = gather_bits(
        jnp.concatenate(
            [log_rate, ssm_coeff, jnp.broadcast_to(ssm_skip[:, None], (rows_h, 128))], axis=1
        ),
        size,
        sorted(top),
        top,
    ).reshape(chans, 1, -1)
    mix_params = (
        params[..., :nstate],
        params[..., nstate : 2 * nstate],
        params[..., 2 * nstate :],
    )
    tables = mixer_tables(*mix_params[:2])
    groups = [[b * group + j for j in range(group)] for b in range(buckets)]

    def exchange(x):
        return lax.all_to_all(x, "dp", split_axis=0, concat_axis=0, axis_index_groups=groups)

    def to_owner(x):
        return exchange(x.reshape(group, chans, tok_chip))

    def from_owner(x):
        return exchange(x).reshape(h_half, tok_chip)

    def swap_turned(x):
        got = swap_cores(x)
        return jnp.concatenate([got[:, tok_dev:], got[:, :tok_dev]], axis=1)

    device = 2 * chip + core
    lane = jnp.arange(tok_dev, dtype=jnp.int32)
    place = jnp.concatenate([device * tok_dev + lane, (device ^ 1) * tok_dev + lane])
    bucket_range = jnp.arange(buckets, dtype=jnp.int32)
    limit = jnp.sum(
        jnp.where((place // SEQ)[:, None] == bucket_range[None, :], lengths[None, :], 0), axis=1
    )
    live = (place % SEQ < limit).astype(F32)[:, None]

    normed, out_grad, reduced_t, two_slope, out_sum = norm_call(
        core_at,
        tok_pair,
        cot_pair,
        jnp.broadcast_to(live, (tok_chip, 128)),
        gain_f,
        nbias_f,
        two_turned,
        jnp.broadcast_to(btwo_f, (h_half, 128)),
    )
    v_seq = to_owner(reduced_t)
    y_seq, entering = mixer_forward(core_at, v_seq, tables, mix_params)
    y_own = from_owner(y_seq)
    y_other = swap_cores(y_own)

    def small_pack(grad_two, gain_sum, nbias_sum, out_sum, one_sum, gate_sum, two_sum):
        def by_device(x):
            return x.reshape(2 * size, -1)

        def by_core(x):
            zero = jnp.zeros_like(x)
            return by_device(natural_pair(x, zero, axis=1))

        grad_btwo = (
            jnp.sum(two_sum, axis=1).reshape(group, buckets, rows_h).swapaxes(0, 1).reshape(size, rows_h)
        )
        vec_grads = jnp.concatenate(
            [
                by_device(gain_sum),
                by_device(nbias_sum),
                by_device(out_sum),
                by_core(one_sum.reshape(size, rows_f)),
                by_core(gate_sum.reshape(size, rows_f)),
                by_core(grad_btwo),
            ],
            axis=1,
        )
        vec_grads = jnp.pad(vec_grads, ((0, 0), (0, vec_rows * h_half - vec_len)))
        return jnp.concatenate(
            [
                grad_two.reshape(2 * size, rows_e, h_half).astype(BF),
                vec_grads.reshape(2 * size, vec_rows, h_half).astype(BF),
            ],
            axis=1,
        )

    act_one, dz_slope, gate_grad, dy_mine, dy_other, gate_sum = early_call(
        core_at, normed, out_grad, bone_f, weights, order
    )
    dy_own = (dy_mine + swap_cores(dy_other).astype(F32)).astype(BF)
    dy_seq = to_owner(dy_own)


    def send_off(sends, low):
        came = {k: across(sends[k - 1], size, k << low) for k in (3, 1, 2)}
        return [came[k] for k in (1, 2, 3)]

    def begin(outputs, have, rest):
        keep, *parts = (x.reshape((2,) * len(have) + rest) for x in outputs)
        return keep, send_off(parts, 0), have

    def split_off(state, low, *others):
        kept, came, have = state
        high = low + 1
        axis = min(have.index(high), have.index(low))
        swapped = have.index(low) < have.index(high)
        shape = kept.shape[:axis] + (4,) + kept.shape[axis + 2 :]
        terms = [kept.reshape(shape)] + [after(x, *others).reshape(shape) for x in came]
        here = (chip >> low) & 3

        def part(k):
            index = here ^ k
            index = ((index & 1) << 1) | (index >> 1) if swapped else index
            return sum(
                lax.dynamic_index_in_dim(x, index, axis, keepdims=False).astype(F32) for x in terms
            )

        return part(0), [part(k).astype(BF) for k in (1, 2, 3)], [b for b in have if b >> 1 != low >> 1]

    def go_on(state, low):
        kept, parts, have = state
        return kept, send_off(parts, low), have

    def to_last(state):
        for low in range(2, bits - 2, 2):
            state = go_on(split_off(state, low), low)
        return state

    def total(state, *others):
        kept, came, _ = state
        return sum((after(x, *others).astype(F32) for x in came), kept)

    here = jnp.reshape(chip & 3, (1,)).astype(jnp.int32)
    last = bits - 2
    far = size // 4
    far_groups = [[4 * g + k for g in range(far)] for k in range(4)]

    product, one_grad, one_sum = gate_call(
        core_at, after(y_own, dy_own), y_other, bthree_f, act_one, dz_slope, weights, order
    )
    grad_four = grad_call(here, product, out_grad, rows_f, 384, "grad_four")
    four = begin(grad_four, natural[:-2], (rows_f, width))
    dv_seq, grad_rate, grad_coeff, grad_skip = mixer_backward(
        core_at, v_seq, after(dy_seq, grad_four[0]), entering, tables, mix_params
    )
    dv_own = from_owner(dv_seq)
    grad_three = mixed_grad_call(
        here, y_own, y_other, after(gate_grad, dv_seq), buckets * rows_h, "grad_three"
    )
    grad_one = grad_call(
        here, normed, after(one_grad, grad_three[0]), 2 * rows_e, 256, "grad_one"
    )

    def stacked(one, three):
        three = three.reshape(2, group // 4, buckets, rows_h, f_half)
        three = jnp.moveaxis(three, (2, 1), (0, 1)).reshape(far, 2 * rows_h, f_half)
        return jnp.concatenate([one.reshape(far, 2 * rows_e, f_half), three], axis=1)

    rest = begin(
        [stacked(x, y) for x, y in zip(grad_one, grad_three)],
        natural[:-2],
        (2 * rows_e + 2 * rows_h, f_half),
    )
    four_parts = total(four, grad_one[0]).astype(BF).reshape(far, rows_f, width)
    four_got = lax.all_to_all(
        after(four_parts, dv_own), "dp", split_axis=0, concat_axis=0, axis_index_groups=far_groups
    )
    out_mine, out_other, one_back = out_call(
        core_at, product, after(one_grad, grad_one[0], dv_own, four_parts), width, weights
    )
    out_got = swap_cores(out_other)
    sum_four = jnp.sum(after(four_got, one_back).astype(F32), axis=0)

    grad_two, back_mine, back_other, gain_sum, nbias_sum, two_sum = tail_call(
        core_at,
        after(dv_own, sum_four),
        two_slope,
        two_turned,
        one_back,
        tok_pair,
        normed,
    )
    mix_grads = jnp.concatenate([grad_rate[:, 0], grad_coeff[:, 0], grad_skip[:, 0]], axis=1)
    mix_grads = scatter_bits(
        mix_grads.reshape((2,) * len(top) + (rows_h, -1)), size, sorted(top)[::-1], top, F32
    )
    back_got = swap_cores(back_other)
    rest = split_off(to_last(rest), last, grad_two)
    rest_sent = rest[1]
    rest = go_on(rest, last)
    small_grads = small_pack(after(grad_two, *rest_sent), gain_sum, nbias_sum, out_sum, one_sum, gate_sum, two_sum)
    small_got = lax.all_to_all(
        small_grads, everyone, split_axis=0, concat_axis=0
    )
    input_grad = input_call(
        core_at, back_mine, after(back_got, small_grads), tokens, out_grad, gain_f
    )


    def merge_f(mine, other):
        rows = mine.shape[0]
        parts = (mine.reshape(rows, size, rows_f), other.reshape(rows, size, rows_f))
        return natural_pair(*parts, axis=2).reshape(rows, 2 * f_half)

    branch = out_mine + after(out_got, small_grads).astype(F32)
    mixed = (live[:tok_dev] * (tokens.astype(F32) + branch + bfour_f)).astype(BF)
    rest_sum = total(rest, input_grad, mixed)
    one_mine, one_other = mine_other(rest_sum[: 2 * rows_e].reshape(2, rows_e, f_half), 0)
    three_sum = rest_sum[2 * rows_e :]
    rest_got = swap_cores(jnp.concatenate([one_other, three_sum[rows_h:]], axis=0))
    merged = merge_f(jnp.concatenate([one_mine, three_sum[:rows_h]], axis=0), rest_got)
    sum_one, sum_three = merged[:rows_e], merged[rows_e:]

    small_sum = jnp.sum(
        after(small_got, input_grad).reshape(size, 2, rows_e + vec_rows, h_half).astype(F32), axis=0
    )
    sum_two = jnp.transpose(
        small_sum[:, :rows_e].reshape(2, rows_e, group, buckets, rows_h), (1, 3, 2, 0, 4)
    ).reshape(rows_e, 2 * h_half)
    vec_sum = jnp.sum(small_sum[:, rows_e:], axis=0).reshape(-1)
    ends = [rows_e, 2 * rows_e, 3 * rows_e, 3 * rows_e + rows_f, 3 * rows_e + 2 * rows_f, vec_len]
    sum_gain, sum_nbias, sum_bfour, sum_bone, sum_bthree, sum_btwo = (
        vec_sum[a:b] for a, b in zip([0] + ends, ends)
    )

    return (
        mixed,
        input_grad,
        sum_gain,
        sum_nbias,
        sum_one,
        sum_bone,
        sum_two,
        sum_btwo,
        sum_three,
        sum_bthree,
        sum_four,
        sum_bfour,
        mix_grads[:, :nstate],
        mix_grads[:, nstate : 2 * nstate],
        mix_grads[:, 2 * nstate],
    )


def solution(mesh):
    both = ("dp", "fsdp")
    rows, vector = P(both, None), P(both)
    in_specs = (
        rows, rows, P(), vector, vector, rows, vector, rows, vector, rows, vector, rows, vector,
        rows, rows, vector,
    )
    out_specs = (
        rows, rows, vector, vector, rows, vector, rows, vector, rows, vector, rows, vector,
        rows, rows, vector,
    )
    return jax.shard_map(
        functools.partial(per_device, mesh.shape["dp"]),
        mesh=mesh,
        in_specs=in_specs,
        out_specs=out_specs,
        check_vma=False,
    )
```

profile of v0, /device:TPU:0, one launch (start us, length us, event | category | flops | bytes accessed | tf_op | source)
XLA Modules:
  0.0 369.6 jit_solution(1497637705939356107)
XLA Ops:
  8.6 1.1 fusion.42
  9.7 1.2 reshape.500
  14.4 7.0 %all-to-all-start = ((bf16[32,34,256]{2,1,0:T(8,128)(2,1)}), bf16[32,34,256]{2,1,0:T(8,128)(2,1)S(1)}, u32[]{:S(2)}, u32[]{:S(2)}) async-start(bf16[32,34,256]{2,1,0:T(8,128)(2,1)} %bitcast.4), calls=%async_computation | async-start | bytes 1310720 | tf_op jit(solution)/shard_map/all_to_all | solution.py:862
  21.8 2.7 collective-permute-start.2
  24.5 1.5 constant_dynamic-update-slice_fusion.1
  26.0 25.7 %all-to-all-done = bf16[32,34,256]{2,1,0:T(8,128)(2,1)S(1)} async-done(((bf16[32,34,256]{2,1,0:T(8,128)(2,1)}), bf16[32,34,256]{2,1,0:T(8,128)(2,1)S(1)}, u32[]{:S(2)}, u32[]{:S(2)}) %all-to-all-start) | async-done | bytes 557088 | tf_op jit(solution)/shard_map/all_to_all | solution.py:862
  52.6 1.2 copy.173
  54.5 3.6 constant_dynamic-update-slice_fusion.tok_ref
  58.2 4.0 %pad_maximum_fusion.cot_ref = bf16[2048,1024]{1,0:T(8,128)(2,1)} fusion(bf16[1024,1024]{1,0:T(8,128)(2,1)} %collective-permute-done.1, bf16[1024,1024]{1,0:T(8,128)(2,1)S(1)} %copy-done.9), kind=kLoop, calls=%fused_computation.4 | loop fusion | flops 8388608 | bytes 8388608 | tf_op jit(solution)/shard_map/concatenate | solution.py:849
  62.3 1.3 broadcast_in_dim.52.live_ref
  63.6 9.5 %norm.1 = (bf16[2048,1024]{1,0:T(8,128)(2,1)}, bf16[2048,1024]{1,0:T(8,128)(2,1)}, bf16[256,2048]{1,0:T(8,128)(2,1)}, bf16[256,2048]{1,0:T(8,128)(2,1)}, f32[1,1024]{1,0:T(1,128)S(1)}) custom-call(s32[1]{0:T(128)} %bitcast._.turn_ref, bf16[2048,1024]{1,0:T(8,128)(2,1)} %constant_dynamic-update-slice_fusion.tok_ref, ...), custom_call_target="tpu_custom_call" | custom-call | flops 9900000256 | bytes 33000000 | tf_op jit(solution)/shard_map/norm/pallas_call | solution.py:320
  73.1 3.7 all-to-all-start.1
  77.0 11.4 %mixer_tables.1 = (bf16[32,256,512]{2,1,0:T(8,128)(2,1)}, bf16[32,512,256]{2,1,0:T(8,128)(2,1)}, bf16[32,256,256]{2,1,0:T(8,128)(2,1)}) custom-call(f32[32,1,512]{2,1,0:T(1,128)S(1)} %get-tuple-element.251.lr_ref, f32[32,1,512]{2,1,0:T(1,128)S(1)} %get-tuple-element.250.co_ref), custom_call_target="tpu_custom_call" | custom-call | flops 11879999488 | bytes 39600000 | tf_op jit(solution)/shard_map/mixer_tables/pallas_call | solution.py:256
  88.5 7.5 %all-to-all-done.1.v_ref = bf16[8,32,2048]{2,1,0:T(8,128)(2,1)S(1)} async-done(((bf16[8,32,2048]{2,1,0:T(8,128)(2,1)}), bf16[8,32,2048]{2,1,0:T(8,128)(2,1)S(1)}, u32[]{:S(2)}, u32[]{:S(2)}) %all-to-all-start.1) | async-done | bytes 1048608 | tf_op jit(solution)/shard_map/all_to_all | solution.py:943
  97.0 13.1 %mixer_forward.1 = (bf16[8,32,2048]{2,1,0:T(8,128)(2,1)}, f32[32,64,512]{2,1,0:T(8,128)}) custom-call(s32[1]{0:T(128)} %bitcast._.turn_ref, bf16[8,32,2048]{2,1,0:T(8,128)(2,1)} %copy-done.11, bf16[32,256,512]{2,1,0:T(8,128)(2,1)} %get-tuple-element.81.d_ref, bf16[32,512,256]{2,1,0:T(8,128)(2,1)} %get-tuple-element.82.dt_ref, ...), custom_call_target="tpu_custom_call" | custom-call | flops 12869999616 | bytes 42900000 | tf_op jit(solution)/shard_map/mixer_forward/pallas_call | solution.py:278
  110.1 4.4 %all-to-all-start.2 = ((bf16[8,32,2048]{2,1,0:T(8,128)(2,1)}), bf16[8,32,2048]{2,1,0:T(8,128)(2,1)S(1)}, u32[]{:S(2)}, u32[]{:S(2)}) async-start(bf16[8,32,2048]{2,1,0:T(8,128)(2,1)} %get-tuple-element.84), calls=%async_computation.2 | async-start | bytes 2097152 | tf_op jit(solution)/shard_map/all_to_all | solution.py:943
  114.5 34.3 %all-gather.3.cloned.1.call-done = bf16[15360,512]{1,0:T(8,128)(2,1)} async-done(((bf16[480,512]{1,0:T(8,128)(2,1)}), bf16[15360,512]{1,0:T(8,128)(2,1)}) %all-gather.3.cloned.1.call-update) | async-done | bytes 15728656 | tf_op jit(solution)/shard_map/all_gather | solution.py:891
  148.8 23.8 %early.1 = (bf16[2048,1536]{1,0:T(8,128)(2,1)}, bf16[2048,1536]{1,0:T(8,128)(2,1)}, bf16[2048,1536]{1,0:T(8,128)(2,1)}, f32[256,2048]{1,0:T(8,128)}, bf16[256,20...) custom-call(s32[1]{0:T(128)} %bitcast._.turn_ref, bf16[2048,1024]{1,0:T(8,128)(2,1)} %get-tuple-element.85.x_ref.a_ref.n_ref, ...), custom_call_target="tpu_custom_call" | custom-call | flops 23759998976 | bytes 79200000 | tf_op jit(solution)/shard_map/early/pallas_call | solution.py:320
  173.7 1.8 collective-permute-done.3
  175.4 3.1 add_convert_fusion
  178.6 4.9 %all-to-all-start.3 = ((bf16[8,32,2048]{2,1,0:T(8,128)(2,1)}), bf16[8,32,2048]{2,1,0:T(8,128)(2,1)}, u32[]{:S(2)}, u32[]{:S(2)}) async-start(bf16[8,32,2048]{2,1,0:T(8,128)(2,1)} %bitcast.21), calls=%async_computation.3 | async-start | bytes 2097152 | tf_op jit(solution)/shard_map/all_to_all | solution.py:943
  183.5 12.6 %gate.1 = (bf16[2048,1536]{1,0:T(8,128)(2,1)}, bf16[2048,1536]{1,0:T(8,128)(2,1)}, f32[1,1536]{1,0:T(1,128)S(1)}) custom-call(s32[1]{0:T(128)} %bitcast._.turn_ref, bf16[256,2048]{1,0:T(8,128)(2,1)S(1)} %bitcast.115, bf16[256,2048]{1,0:T(8,128)(2,1)} %collective-permute-done.4.yo_ref, f32[1,1536]{1,0:T(1,128)S(1)} %reshape.505.b3_ref, ...), custom_call_target="tpu_custom_call" | custom-call | flops 12869999616 | bytes 42900000 | tf_op jit(solution)/shard_map/gate/pallas_call | solution.py:320
  196.3 11.1 %grad_four.1 = (f32[384,1024]{1,0:T(8,128)}, bf16[384,1024]{1,0:T(8,128)(2,1)S(1)}, bf16[384,1024]{1,0:T(8,128)(2,1)S(1)}, bf16[384,1024]{1,0:T(8,128)(2,1)}) custom-call(s32[1]{0:T(128)} %bitcast.20.here_ref, bf16[2048,1536]{1,0:T(8,128)(2,1)} %get-tuple-element.92.a_ref.z_ref, bf16[2048,1024]{1,0:T(8,128)(2,1)} %get-tuple-element.86.g_ref.b_ref), custom_call_target="tpu_custom_call" | custom-call | flops 10890000384 | bytes 36300000 | tf_op jit(solution)/shard_map/grad_four/pallas_call | solution.py:320
  207.4 2.0 collective-permute-start.6
  209.4 1.5 collective-permute-start.5
  211.0 19.8 %mixer_backward.1 = (bf16[8,32,2048]{2,1,0:T(8,128)(2,1)}, f32[32,1,512]{2,1,0:T(1,128)S(1)}, f32[32,1,512]{2,1,0:T(1,128)S(1)}, f32[32,1,128]{2,1,0:T(1,128)S(1)}) custom-call(s32[1]{0:T(128)} %bitcast._.turn_ref, bf16[8,32,2048]{2,1,0:T(8,128)(2,1)} %copy-done.11, bf16[8,32,2048]{2,1,0:T(8,128)(2,1)} %all-to-all-done.3.dy_ref, ...), custom_call_target="tpu_custom_call" | custom-call | flops 19800000512 | bytes 66000000 | tf_op jit(solution)/shard_map/mixer_backward/pallas_call | solution.py:278
  230.8 5.1 %all-to-all-start.4 = ((bf16[8,32,2048]{2,1,0:T(8,128)(2,1)}), bf16[8,32,2048]{2,1,0:T(8,128)(2,1)}, u32[]{:S(2)}, u32[]{:S(2)}) async-start(bf16[8,32,2048]{2,1,0:T(8,128)(2,1)} %get-tuple-element.98), calls=%async_computation.4 | async-start | bytes 2097152 | tf_op jit(solution)/shard_map/all_to_all | solution.py:943
  235.9 6.5 %grad_three.1 = (f32[128,1536]{1,0:T(8,128)S(1)}, bf16[128,1536]{1,0:T(8,128)(2,1)S(1)}, bf16[128,1536]{1,0:T(8,128)(2,1)S(1)}, bf16[128,1536]{1,0:T(8,128)(2,1)S(1)}) custom-call(s32[1]{0:T(128)} %bitcast.20.here_ref, bf16[256,2048]{1,0:T(8,128)(2,1)} %bitcast.116, bf16[256,2048]{1,0:T(8,128)(2,1)} %collective-permute-done.4.yo_ref, ...), custom_call_target="tpu_custom_call" | custom-call | flops 7920000000 | bytes 26400000 | tf_op jit(solution)/shard_map/grad_three/pallas_call | solution.py:320
  242.4 11.6 %grad_one.1 = (f32[256,1536]{1,0:T(8,128)}, bf16[256,1536]{1,0:T(8,128)(2,1)S(1)}, bf16[256,1536]{1,0:T(8,128)(2,1)S(1)}, bf16[256,1536]{1,0:T(8,128)(2,1)}) custom-call(s32[1]{0:T(128)} %bitcast.20.here_ref, bf16[2048,1024]{1,0:T(8,128)(2,1)} %get-tuple-element.85.x_ref.a_ref.n_ref, bf16[2048,1536]{1,0:T(8,128)(2,1)} %get-tuple-element.109.b_ref.dh_ref), custom_call_target="tpu_custom_call" | custom-call | flops 11879999488 | bytes 39600000 | tf_op jit(solution)/shard_map/grad_one/pallas_call | solution.py:320
  255.2 1.1 pad_maximum_fusion.3
  256.3 2.9 collective-permute-start.11
  259.2 1.1 pad_maximum_fusion.2
  260.9 1.1 pad_maximum_fusion.1
  262.0 3.1 add_convert_fusion.1
  265.1 5.2 %all-to-all-start.5 = ((bf16[4,96,1024]{2,1,0:T(8,128)(2,1)}), bf16[4,96,1024]{2,1,0:T(8,128)(2,1)S(1)}, u32[]{:S(2)}, u32[]{:S(2)}) async-start(bf16[4,96,1024]{2,1,0:T(8,128)(2,1)} %bitcast.27), calls=%async_computation.5 | async-start | bytes 1572864 | tf_op jit(solution)/shard_map/all_to_all | solution.py:1088
  270.3 20.1 %out.1 = (f32[1024,1024]{1,0:T(8,128)}, bf16[1024,1024]{1,0:T(8,128)(2,1)}, bf16[2048,1024]{1,0:T(8,128)(2,1)}) custom-call(s32[1]{0:T(128)} %bitcast._.turn_ref, bf16[2048,1536]{1,0:T(8,128)(2,1)} %get-tuple-element.92.a_ref.z_ref, bf16[2048,1536]{1,0:T(8,128)(2,1)} %get-tuple-element.109.b_ref.dh_ref, bf16[16,2,480,512]{3,2,1,0:T(8,128)(2,1)} %bitcast.175, ...), custom_call_target="tpu_custom_call" | custom-call | flops 19800000512 | bytes 66000000 | tf_op jit(solution)/shard_map/out/pallas_call | solution.py:320
  290.4 2.9 collective-permute-start.17
  294.4 11.1 %tail.1 = (bf16[1024,256]{1,0:T(8,128)(2,1)S(1)}, f32[1024,1024]{1,0:T(8,128)}, bf16[1024,1024]{1,0:T(8,128)(2,1)}, f32[1,1024]{1,0:T(1,128)S(1)}, f32[1,1024]{1,0:T(1,128)S(1)}, /*index=5*/f32[256,128]{1,0:T(8,128)S(1)}) custom-call(s32[1]{0:T(128)} %bitcast._.turn_ref, bf16[256,2048]{1,0:T(8,128)(2,1)} %bitcast.22.dv_ref, ...), custom_call_target="tpu_custom_call" | custom-call | flops 990000000 | bytes 3300000 | tf_op jit(solution)/shard_map/tail/pallas_call | solution.py:320
  307.0 2.2 collective-permute-done.10
  309.6 2.9 fusion.24
  312.5 3.6 collective-permute-start.15
  318.5 5.9 %all-to-all-start.6 = ((bf16[32,34,256]{2,1,0:T(8,128)(2,1)}), bf16[32,34,256]{2,1,0:T(8,128)(2,1)S(1)}, u32[]{:S(2)}, u32[]{:S(2)}) async-start(bf16[32,34,256]{2,1,0:T(8,128)(2,1)} %pad_maximum_fusion.4), calls=%async_computation.6 | async-start | bytes 1310720 | tf_op jit(solution)/shard_map/all_to_all | solution.py:1115
  324.5 5.2 %multiply_convert_fusion = bf16[1024,1024]{1,0:T(8,128)(2,1)} fusion(f32[1024,1024]{1,0:T(8,128)} %get-tuple-element.110, bf16[1024,1024]{1,0:T(8,128)(2,1)} %collective-permute-done.8, bf16[1024,1024]{1,0:T(8,128)(2,1)S(1)} %copy-done.4, f32[1024]{0:T(1024)S(1)} %add.207, f32[1024]{0:T(1024)S(1)} %slice-done), kind=kLoop, calls=%fused_computation.5 | loop fusion | flops 7340032 | bytes 10493952 | tf_op jit(solution)/shard_map/convert_element_type | solution.py:1129
  329.7 7.1 %input_grad.1 = bf16[1024,1024]{1,0:T(8,128)(2,1)} custom-call(s32[1]{0:T(128)} %bitcast._.turn_ref, f32[1024,1024]{1,0:T(8,128)} %get-tuple-element.135.mine_ref, bf16[1024,1024]{1,0:T(8,128)(2,1)} %collective-permute-done.12.got_ref, bf16[1024,1024]{1,0:T(8,128)(2,1)} %tok_ref.1, bf16[2048,1024]{1,0:T(8,128)(2,1)} %get-tuple-element.86.g_ref.b_ref, ...), custom_call_target="tpu_custom_call" | custom-call | flops 6929999872 | bytes 23100000 | tf_op jit(solution)/shard_map/input_grad/pallas_call | solution.py:320
  336.8 12.8 %collective-permute-done.14 = bf16[96,1536]{1,0:T(8,128)(2,1)} collective-permute-done((bf16[96,1536]{1,0:T(8,128)(2,1)}, bf16[96,1536]{1,0:T(8,128)(2,1)}, u32[]{:S(2)}, u32[]{:S(2)}) %collective-permute-start.14) | collective-permute-done | bytes 294944 | tf_op jit(solution)/shard_map/ppermute | solution.py:766
  349.6 1.6 fusion.7
  351.3 4.8 %all-to-all-done.6 = bf16[32,34,256]{2,1,0:T(8,128)(2,1)S(1)} async-done(((bf16[32,34,256]{2,1,0:T(8,128)(2,1)}), bf16[32,34,256]{2,1,0:T(8,128)(2,1)S(1)}, u32[]{:S(2)}, u32[]{:S(2)}) %all-to-all-start.6) | async-done | bytes 557088 | tf_op jit(solution)/shard_map/all_to_all | solution.py:1115
  360.3 1.4 slice.145
  (189 shorter events, 21.6 us)
Async XLA Ops:
  7.2 141.6 %all-gather.3.cloned.1.call-start = ((), (), s32[]{:S(2)}) async-start(), calls=%async_computation.7 | async-start | bytes 16220160 | tf_op jit(solution)/shard_map/all_gather | solution.py:891
  8.5 3.7 %copy-start.3 = (bf16[1024,1024]{1,0:T(8,128)(2,1)S(1)}, bf16[1024,1024]{1,0:T(8,128)(2,1)}, u32[]{:S(2)}) copy-start(bf16[1024,1024]{1,0:T(8,128)(2,1)} %tok_ref.1) | copy-start | bytes 6291460
  8.5 4.3 %copy-start.19 = (bf16[32]{0:T(256)(128)(2,1)S(1)}, bf16[32]{0:T(256)(128)(2,1)}, u32[]{:S(2)}) copy-start(bf16[32]{0:T(256)(128)(2,1)} %param.19) | copy-start | bytes 196
  8.5 4.3 %copy-start.20 = (bf16[32]{0:T(256)(128)(2,1)S(1)}, bf16[32]{0:T(256)(128)(2,1)}, u32[]{:S(2)}) copy-start(bf16[32]{0:T(256)(128)(2,1)} %param.20) | copy-start | bytes 196
  8.5 4.2 %copy-start.21 = (bf16[32]{0:T(256)(128)(2,1)S(1)}, bf16[32]{0:T(256)(128)(2,1)}, u32[]{:S(2)}) copy-start(bf16[32]{0:T(256)(128)(2,1)} %param.28) | copy-start | bytes 196
  8.6 4.2 %copy-start.22 = (bf16[96]{0:T(256)(128)(2,1)S(1)}, bf16[96]{0:T(256)(128)(2,1)}, u32[]{:S(2)}) copy-start(bf16[96]{0:T(256)(128)(2,1)} %param.22) | copy-start | bytes 580
  8.6 4.2 %copy-start.23 = (bf16[96]{0:T(256)(128)(2,1)S(1)}, bf16[96]{0:T(256)(128)(2,1)}, u32[]{:S(2)}) copy-start(bf16[96]{0:T(256)(128)(2,1)} %param.26) | copy-start | bytes 580
  8.6 4.2 %copy-start.24 = (bf16[16]{0:T(256)(128)(2,1)S(1)}, bf16[16]{0:T(256)(128)(2,1)}, u32[]{:S(2)}) copy-start(bf16[16]{0:T(256)(128)(2,1)} %param.24) | copy-start | bytes 100
  8.6 4.5 %copy-start.16 = (bf16[32,512]{1,0:T(8,128)(2,1)S(1)}, bf16[32,512]{1,0:T(8,128)(2,1)}, u32[]{:S(2)}) copy-start(bf16[32,512]{1,0:T(8,128)(2,1)} %param.23) | copy-start | bytes 98308
  12.2 9.4 %copy-start.17 = (f32[16]{0:T(128)S(1)}, f32[16]{0:T(128)}, u32[]{:S(2)}) copy-start(f32[16]{0:T(128)} %param.31) | copy-start | bytes 196
  12.2 9.5 %copy-start.13 = (f32[16,512]{1,0:T(8,128)S(1)}, f32[16,512]{1,0:T(8,128)}, u32[]{:S(2)}) copy-start(f32[16,512]{1,0:T(8,128)} %param.30) | copy-start | bytes 98308
  12.2 9.5 %copy-start.14 = (f32[16,512]{1,0:T(8,128)S(1)}, f32[16,512]{1,0:T(8,128)}, u32[]{:S(2)}) copy-start(f32[16,512]{1,0:T(8,128)} %param.29) | copy-start | bytes 98308
  12.2 12.2 %copy-start.18 = (s32[2]{0:T(128)S(1)}, s32[2]{0:T(128)}, u32[]{:S(2)}) copy-start(s32[2]{0:T(128)} %param.18) | copy-start | bytes 28
  12.3 42.2 %collective-permute-start = (bf16[1024,1024]{1,0:T(8,128)(2,1)S(1)}, bf16[1024,1024]{1,0:T(8,128)(2,1)}, u32[]{:S(2)}, u32[]{:S(2)}) collective-permute-start(bf16[1024,1024]{1,0:T(8,128)(2,1)S(1)} %copy-done.3), channel_id=1, source_target_pairs={{0,1},{1,0},{2,3},{3,2},{4,5},{5,4},{6,7},{7,6},{8,9},{9,8},{10,11... | collective-permute-start | bytes 6291464 | tf_op jit(solution)/shard_map/ppermute | solution.py:762
  14.4 37.4 %all-to-all-start = ((bf16[32,34,256]{2,1,0:T(8,128)(2,1)}), bf16[32,34,256]{2,1,0:T(8,128)(2,1)S(1)}, u32[]{:S(2)}, u32[]{:S(2)}) async-start(bf16[32,34,256]{2,1,0:T(8,128)(2,1)} %bitcast.4), calls=%async_computation | async-start | bytes 1310720 | tf_op jit(solution)/shard_map/all_to_all | solution.py:862
  21.4 36.8 %collective-permute-start.1 = (bf16[1024,1024]{1,0:T(8,128)(2,1)}, bf16[1024,1024]{1,0:T(8,128)(2,1)}, u32[]{:S(2)}, u32[]{:S(2)}) collective-permute-start(bf16[1024,1024]{1,0:T(8,128)(2,1)} %param.17), channel_id=1, source_target_pairs={{0,1},{1,0},{2,3},{3,2},{4,5},{5,4},{6,7},{7,6},{8,9},{9,8},{10,11... | collective-permute-start | bytes 6291464 | tf_op jit(solution)/shard_map/ppermute | solution.py:762
  21.8 55.0 %collective-permute-start.2 = (f32[16,1152]{1,0:T(8,128)S(1)}, f32[16,1152]{1,0:T(8,128)S(1)}, u32[]{:S(2)}, u32[]{:S(2)}) collective-permute-start(f32[16,1152]{1,0:T(8,128)S(1)} %pad_maximum_fusion.12), channel_id=1, source_target_pairs={{0,16},{2,18},{4,20},{6,22},{8,24},{10,26},{12,28},{14,30},{16,0},... | collective-permute-start | bytes 221192 | tf_op jit(solution)/shard_map/ppermute | solution.py:766
  26.0 147.1 %copy-start.15 = (f32[2048]{0:T(1024)}, f32[2048]{0:T(1024)S(1)}, u32[]{:S(2)}) copy-start(f32[2048]{0:T(1024)S(1)} %fusion.32) | copy-start | bytes 24580
  54.3 9.3 %copy-start.1 = (f32[1,1024]{1,0:T(1,128)}, f32[1,1024]{1,0:T(1,128)S(1)}, u32[]{:S(2)}) copy-start(f32[1,1024]{1,0:T(1,128)S(1)} %reshape.491.gain_ref) | copy-start | bytes 12292
  73.1 23.0 %all-to-all-start.1 = ((bf16[8,32,2048]{2,1,0:T(8,128)(2,1)}), bf16[8,32,2048]{2,1,0:T(8,128)(2,1)S(1)}, u32[]{:S(2)}, u32[]{:S(2)}) async-start(bf16[8,32,2048]{2,1,0:T(8,128)(2,1)} %bitcast.9), calls=%async_computation.1 | async-start | bytes 2097152 | tf_op jit(solution)/shard_map/all_to_all | solution.py:943
  110.1 62.8 %all-to-all-start.2 = ((bf16[8,32,2048]{2,1,0:T(8,128)(2,1)}), bf16[8,32,2048]{2,1,0:T(8,128)(2,1)S(1)}, u32[]{:S(2)}, u32[]{:S(2)}) async-start(bf16[8,32,2048]{2,1,0:T(8,128)(2,1)} %get-tuple-element.84), calls=%async_computation.2 | async-start | bytes 2097152 | tf_op jit(solution)/shard_map/all_to_all | solution.py:943
  172.6 2.8 collective-permute-start.3
  172.9 10.6 %copy-start = (bf16[8,32,2048]{2,1,0:T(8,128)(2,1)}, bf16[8,32,2048]{2,1,0:T(8,128)(2,1)S(1)}, u32[]{:S(2)}) copy-start(bf16[8,32,2048]{2,1,0:T(8,128)(2,1)S(1)} %all-to-all-done.2) | copy-start | bytes 3145732
  172.9 10.6 %collective-permute-start.4 = (bf16[256,2048]{1,0:T(8,128)(2,1)S(1)}, bf16[256,2048]{1,0:T(8,128)(2,1)}, u32[]{:S(2)}, u32[]{:S(2)}) collective-permute-start(bf16[256,2048]{1,0:T(8,128)(2,1)S(1)} %bitcast.114), channel_id=1, source_target_pairs={{0,1},{1,0},{2,3},{3,2},{4,5},{5,4},{6,7},{7,6},{8,9},{9,8},{10,11... | collective-permute-start | bytes 3145736 | tf_op jit(solution)/shard_map/ppermute | solution.py:762
  178.6 32.4 %all-to-all-start.3 = ((bf16[8,32,2048]{2,1,0:T(8,128)(2,1)}), bf16[8,32,2048]{2,1,0:T(8,128)(2,1)}, u32[]{:S(2)}, u32[]{:S(2)}) async-start(bf16[8,32,2048]{2,1,0:T(8,128)(2,1)} %bitcast.21), calls=%async_computation.3 | async-start | bytes 2097152 | tf_op jit(solution)/shard_map/all_to_all | solution.py:943
  207.4 46.7 %collective-permute-start.6 = (bf16[2,2,96,1024]{3,2,1,0:T(8,128)(2,1)S(1)}, bf16[2,2,96,1024]{3,2,1,0:T(8,128)(2,1)}, u32[]{:S(2)}, u32[]{:S(2)}) collective-permute-start(bf16[2,2,96,1024]{3,2,1,0:T(8,128)(2,1)S(1)} %bitcast.126), channel_id=1, source_target_pairs={{0,4},{2,6},{4,0},{6,2},{8,12},{10,14},{12,8},{14,10},{16,20},{18,... | collective-permute-start | bytes 2359304 | tf_op jit(solution)/shard_map/ppermute | solution.py:766
  209.4 44.7 %collective-permute-start.5 = (bf16[2,2,96,1024]{3,2,1,0:T(8,128)(2,1)S(1)}, bf16[2,2,96,1024]{3,2,1,0:T(8,128)(2,1)}, u32[]{:S(2)}, u32[]{:S(2)}) collective-permute-start(bf16[2,2,96,1024]{3,2,1,0:T(8,128)(2,1)S(1)} %bitcast.125), channel_id=1, source_target_pairs={{0,2},{2,0},{4,6},{6,4},{8,10},{10,8},{12,14},{14,12},{16,18},{18,... | collective-permute-start | bytes 2359304 | tf_op jit(solution)/shard_map/ppermute | solution.py:766
  210.9 43.3 %collective-permute-start.7 = (bf16[2,2,96,1024]{3,2,1,0:T(8,128)(2,1)}, bf16[2,2,96,1024]{3,2,1,0:T(8,128)(2,1)}, u32[]{:S(2)}, u32[]{:S(2)}) collective-permute-start(bf16[2,2,96,1024]{3,2,1,0:T(8,128)(2,1)} %bitcast.177), channel_id=1, source_target_pairs={{0,6},{2,4},{4,2},{6,0},{8,14},{10,12},{12,10},{14,8},{16,22},{18,... | collective-permute-start | bytes 2359304 | tf_op jit(solution)/shard_map/ppermute | solution.py:766
  230.8 34.3 %all-to-all-start.4 = ((bf16[8,32,2048]{2,1,0:T(8,128)(2,1)}), bf16[8,32,2048]{2,1,0:T(8,128)(2,1)}, u32[]{:S(2)}, u32[]{:S(2)}) async-start(bf16[8,32,2048]{2,1,0:T(8,128)(2,1)} %get-tuple-element.98), calls=%async_computation.4 | async-start | bytes 2097152 | tf_op jit(solution)/shard_map/all_to_all | solution.py:943
  256.3 50.8 %collective-permute-start.11 = (bf16[2,2,96,1536]{3,2,1,0:T(8,128)(2,1)}, bf16[2,2,96,1536]{3,2,1,0:T(8,128)(2,1)}, u32[]{:S(2)}, u32[]{:S(2)}) collective-permute-start(bf16[2,2,96,1536]{3,2,1,0:T(8,128)(2,1)} %pad_maximum_fusion.3), channel_id=1, source_target_pairs={{0,6},{2,4},{4,2},{6,0},{8,14},{10,12},{12,10},{14,8},{16,22},{18,... | collective-permute-start | bytes 3538952 | tf_op jit(solution)/shard_map/ppermute | solution.py:766
  260.3 48.9 %collective-permute-start.10 = (bf16[2,2,96,1536]{3,2,1,0:T(8,128)(2,1)}, bf16[2,2,96,1536]{3,2,1,0:T(8,128)(2,1)}, u32[]{:S(2)}, u32[]{:S(2)}) collective-permute-start(bf16[2,2,96,1536]{3,2,1,0:T(8,128)(2,1)} %pad_maximum_fusion.2), channel_id=1, source_target_pairs={{0,4},{2,6},{4,0},{6,2},{8,12},{10,14},{12,8},{14,10},{16,20},{18,... | collective-permute-start | bytes 3538952 | tf_op jit(solution)/shard_map/ppermute | solution.py:766
  262.0 47.6 %collective-permute-start.9 = (bf16[2,2,96,1536]{3,2,1,0:T(8,128)(2,1)}, bf16[2,2,96,1536]{3,2,1,0:T(8,128)(2,1)}, u32[]{:S(2)}, u32[]{:S(2)}) collective-permute-start(bf16[2,2,96,1536]{3,2,1,0:T(8,128)(2,1)} %pad_maximum_fusion.1), channel_id=1, source_target_pairs={{0,2},{2,0},{4,6},{6,4},{8,10},{10,8},{12,14},{14,12},{16,18},{18,... | collective-permute-start | bytes 3538952 | tf_op jit(solution)/shard_map/ppermute | solution.py:766
  265.1 28.4 %all-to-all-start.5 = ((bf16[4,96,1024]{2,1,0:T(8,128)(2,1)}), bf16[4,96,1024]{2,1,0:T(8,128)(2,1)S(1)}, u32[]{:S(2)}, u32[]{:S(2)}) async-start(bf16[4,96,1024]{2,1,0:T(8,128)(2,1)} %bitcast.27), calls=%async_computation.5 | async-start | bytes 1572864 | tf_op jit(solution)/shard_map/all_to_all | solution.py:1088
  290.4 34.0 %collective-permute-start.8 = (bf16[1024,1024]{1,0:T(8,128)(2,1)}, bf16[1024,1024]{1,0:T(8,128)(2,1)}, u32[]{:S(2)}, u32[]{:S(2)}) collective-permute-start(bf16[1024,1024]{1,0:T(8,128)(2,1)} %get-tuple-element.111), channel_id=1, source_target_pairs={{0,1},{1,0},{2,3},{3,2},{4,5},{5,4},{6,7},{7,6},{8,9},{9,8},{10,11... | collective-permute-start | bytes 6291464 | tf_op jit(solution)/shard_map/ppermute | solution.py:762
  290.4 15.1 %collective-permute-start.17 = (f32[16,1152]{1,0:T(8,128)S(1)}, f32[16,1152]{1,0:T(8,128)S(1)}, u32[]{:S(2)}, u32[]{:S(2)}) collective-permute-start(f32[16,1152]{1,0:T(8,128)S(1)} %dynamic-slice_bitcast_fusion), channel_id=1, source_target_pairs={{0,16},{2,18},{4,20},{6,22},{8,24},{10,26},{12,28},{14,30},{16,0},... | collective-permute-start | bytes 221192 | tf_op jit(solution)/shard_map/ppermute | solution.py:766
  293.4 16.1 %copy-start.5 = (f32[2,2,2,16,1536]{4,3,2,1,0:T(8,128)}, f32[2,2,2,16,1536]{4,3,2,1,0:T(8,128)S(1)}, u32[]{:S(2)}) copy-start(f32[2,2,2,16,1536]{4,3,2,1,0:T(8,128)S(1)} %copy.179) | copy-start | bytes 2359300
  294.4 15.1 %copy-start.7 = (f32[256,1536]{1,0:T(8,128)S(1)}, f32[256,1536]{1,0:T(8,128)}, u32[]{:S(2)}) copy-start(f32[256,1536]{1,0:T(8,128)} %get-tuple-element.102) | copy-start | bytes 4718596
  305.5 24.1 %collective-permute-start.12 = (bf16[1024,1024]{1,0:T(8,128)(2,1)}, bf16[1024,1024]{1,0:T(8,128)(2,1)}, u32[]{:S(2)}, u32[]{:S(2)}) collective-permute-start(bf16[1024,1024]{1,0:T(8,128)(2,1)} %get-tuple-element.136), channel_id=1, source_target_pairs={{0,1},{1,0},{2,3},{3,2},{4,5},{5,4},{6,7},{7,6},{8,9},{9,8},{10,11... | collective-permute-start | bytes 6291464 | tf_op jit(solution)/shard_map/ppermute | solution.py:762
  312.5 12.0 %copy-start.4 = (bf16[1024,1024]{1,0:T(8,128)(2,1)S(1)}, bf16[1024,1024]{1,0:T(8,128)(2,1)}, u32[]{:S(2)}) copy-start(bf16[1024,1024]{1,0:T(8,128)(2,1)} %tok_ref.1) | copy-start | bytes 6291460
  312.5 12.0 %slice-start = ((f32[2048]{0:T(1024)}), f32[1024]{0:T(1024)S(1)}, s32[]{:S(2)}) async-start(f32[2048]{0:T(1024)} %copy-done.15), calls=%async_computation.8 | async-start | bytes 8192 | tf_op jit(solution)/shard_map/slice | solution.py:1129
  312.5 24.3 %collective-permute-start.15 = (bf16[96,1536]{1,0:T(8,128)(2,1)}, bf16[96,1536]{1,0:T(8,128)(2,1)}, u32[]{:S(2)}, u32[]{:S(2)}) collective-permute-start(bf16[96,1536]{1,0:T(8,128)(2,1)} %get-tuple-element.239), channel_id=1, source_target_pairs={{0,24},{2,26},{4,28},{6,30},{8,16},{10,18},{12,20},{14,22},{16,8},... | collective-permute-start | bytes 884744 | tf_op jit(solution)/shard_map/ppermute | solution.py:766
  316.1 33.5 %collective-permute-start.14 = (bf16[96,1536]{1,0:T(8,128)(2,1)}, bf16[96,1536]{1,0:T(8,128)(2,1)}, u32[]{:S(2)}, u32[]{:S(2)}) collective-permute-start(bf16[96,1536]{1,0:T(8,128)(2,1)} %get-tuple-element.240), channel_id=1, source_target_pairs={{0,16},{2,18},{4,20},{6,22},{8,24},{10,26},{12,28},{14,30},{16,0},... | collective-permute-start | bytes 884744 | tf_op jit(solution)/shard_map/ppermute | solution.py:766
  316.1 33.5 %collective-permute-start.13 = (bf16[96,1536]{1,0:T(8,128)(2,1)}, bf16[96,1536]{1,0:T(8,128)(2,1)}, u32[]{:S(2)}, u32[]{:S(2)}) collective-permute-start(bf16[96,1536]{1,0:T(8,128)(2,1)} %get-tuple-element.241), channel_id=1, source_target_pairs={{0,8},{2,10},{4,12},{6,14},{8,0},{10,2},{12,4},{14,6},{16,24},{18,... | collective-permute-start | bytes 884744 | tf_op jit(solution)/shard_map/ppermute | solution.py:766
  318.5 37.6 %all-to-all-start.6 = ((bf16[32,34,256]{2,1,0:T(8,128)(2,1)}), bf16[32,34,256]{2,1,0:T(8,128)(2,1)S(1)}, u32[]{:S(2)}, u32[]{:S(2)}) async-start(bf16[32,34,256]{2,1,0:T(8,128)(2,1)} %pad_maximum_fusion.4), calls=%async_computation.6 | async-start | bytes 1310720 | tf_op jit(solution)/shard_map/all_to_all | solution.py:1115
  324.5 5.2 %copy-start.2 = (f32[1,1024]{1,0:T(1,128)S(1)}, f32[1,1024]{1,0:T(1,128)}, u32[]{:S(2)}) copy-start(f32[1,1024]{1,0:T(1,128)} %copy-done.1) | copy-start | bytes 12292
  329.7 19.9 %copy-start.6 = (f32[2,2,2,16,1536]{4,3,2,1,0:T(8,128)S(1)}, f32[2,2,2,16,1536]{4,3,2,1,0:T(8,128)}, u32[]{:S(2)}) copy-start(f32[2,2,2,16,1536]{4,3,2,1,0:T(8,128)} %copy-done.5) | copy-start | bytes 2359300
  329.7 19.9 %copy-start.8 = (f32[256,1536]{1,0:T(8,128)S(1)}, f32[256,1536]{1,0:T(8,128)}, u32[]{:S(2)}) copy-start(f32[256,1536]{1,0:T(8,128)} %get-tuple-element.102) | copy-start | bytes 4718596
  356.3 2.8 collective-permute-start.16
  (4 other events, 8.6 us)
Sparse Core Ops, SparseCore 0:
  12.4 136.3 all-gather.2
where the time goes:
time: 371 us; the launch traced here: 370 us
  Pallas kernels  158 us (43%)
  waiting for transfers between devices  89.5 us (24%)
  starting transfers between devices  54.8 us (15%)
  other arithmetic  27.8 us (7%)
  local copies, waits for them, and re-layouts  24.9 us (7%)
  between operations  14.8 us (4%)
    pallas_call x9, Pallas kernels, call(): pl.pallas_call(kernel, grid_spec=pltpu.PrefetchScalarGridSpec(num_scalar_...  113 us
    all_gather x1, waiting for transfers between devices, per_device(): gathered = lax.all_gather(packed, everyone, axis=0)  34.3 us
    pallas_call x2, Pallas kernels, mixer_call(): pl.pallas_call(kernel, grid_spec=pltpu.PrefetchScalarGridSpec(num_scalar_...  32.9 us
    all_to_all x1, waiting for transfers between devices, per_device(): lax.all_to_all(small.reshape((2 * size,) + small.shape[2:]), everyone, sp...  25.7 us
    all_to_all x4, starting transfers between devices, exchange(): lax.all_to_all(x, 'dp', split_axis=0, concat_axis=0, axis_index_groups=gr...  18 us
    ppermute x11, starting transfers between devices, across(): return lax.ppermute(x, 'dp', [(i, i ^ flip) for i in range(size)])  17 us
    ppermute x11, waiting for transfers between devices, across(): return lax.ppermute(x, 'dp', [(i, i ^ flip) for i in range(size)])  15.4 us
    pallas_call x1, Pallas kernels, mixer_tables(): pl.pallas_call(table_kernel, grid=(chans // per,), in_specs=[spec(1, n)]...  11.4 us
  transfers between devices with their start and end apart: 26, of which 8 were waited for; matrix products, arithmetic and copies ran while one was open for 11% of the time, Pallas kernels for 43%

commit v1 on v0

--- a/solution.py
+++ b/solution.py
@@ -550,10 +550,11 @@
 
 def gate_call(core, y_mine, y_other, b3, u, dzs, weights, order):
     tokens, cols = u.shape
-    wide, tall = (TILE, cols), (y_mine.shape[0], TILE)
+    tile = 2 * TILE
+    wide, tall = (tile, cols), (y_mine.shape[0], tile)
     return call(
         functools.partial(gate_kernel, order=order),
-        tokens // TILE,
+        tokens // tile,
         core,
         [
             (y_mine, tall, col_tile),

time: 371 us -> 378 us (1.019)
  starting transfers between devices: 54.8 us -> 60.6 us
    all_to_all x1, starting transfers between devices: 5.21 us -> 12.8 us  [per_device(): lax.all_to_all(after(four_parts, dv_own), 'dp', split_axis=0, concat_axis...]
  transfers between devices with their start and end apart: 26 -> 26, of which waited for: 8 -> 6; matrix products, arithmetic and copies ran while one was open for 11% -> 11% of each run, Pallas kernels for 43% -> 42%
where the time goes in v1:
time: 378 us; the launch traced here: 374 us
  Pallas kernels  156 us (41%)
  waiting for transfers between devices  88.9 us (24%)
  starting transfers between devices  60.6 us (16%)
  other arithmetic  27.8 us (7%)
  local copies, waits for them, and re-layouts  24.9 us (7%)
  between operations  15 us (4%)
    pallas_call x9, Pallas kernels, call(): pl.pallas_call(kernel, grid_spec=pltpu.PrefetchScalarGridSpec(num_scalar_...  112 us
    all_gather x1, waiting for transfers between devices, per_device(): gathered = lax.all_gather(packed, everyone, axis=0)  34 us
    pallas_call x2, Pallas kernels, mixer_call(): pl.pallas_call(kernel, grid_spec=pltpu.PrefetchScalarGridSpec(num_scalar_...  32.9 us
    all_to_all x1, waiting for transfers between devices, per_device(): lax.all_to_all(small.reshape((2 * size,) + small.shape[2:]), everyone, sp...  25.7 us
    all_to_all x4, starting transfers between devices, exchange(): lax.all_to_all(x, 'dp', split_axis=0, concat_axis=0, axis_index_groups=gr...  18.4 us
    ppermute x11, starting transfers between devices, across(): return lax.ppermute(x, 'dp', [(i, i ^ flip) for i in range(size)])  17.1 us
    ppermute x11, waiting for transfers between devices, across(): return lax.ppermute(x, 'dp', [(i, i ^ flip) for i in range(size)])  15.1 us
    all_to_all x1, starting transfers between devices, per_device(): lax.all_to_all(after(four_parts, dv_own), 'dp', split_axis=0, concat_axis...  12.8 us
  transfers between devices with their start and end apart: 26, of which 6 were waited for; matrix products, arithmetic and copies ran while one was open for 11% of the time, Pallas kernels for 42%

profile of v1, /device:TPU:0, one launch (start us, length us, event | category | flops | bytes accessed | tf_op | source)
XLA Modules:
  0.0 373.6 jit_solution(14314739967228447513)
XLA Ops:
  9.7 1.2 reshape.500
  14.4 7.0 %all-to-all-start = ((bf16[32,34,256]{2,1,0:T(8,128)(2,1)}), bf16[32,34,256]{2,1,0:T(8,128)(2,1)S(1)}, u32[]{:S(2)}, u32[]{:S(2)}) async-start(bf16[32,34,256]{2,1,0:T(8,128)(2,1)} %bitcast.4), calls=%async_computation | async-start | bytes 1310720 | tf_op jit(solution)/shard_map/all_to_all | solution.py:863
  21.8 2.7 collective-permute-start.2
  24.5 1.5 constant_dynamic-update-slice_fusion.1
  26.0 25.7 %all-to-all-done = bf16[32,34,256]{2,1,0:T(8,128)(2,1)S(1)} async-done(((bf16[32,34,256]{2,1,0:T(8,128)(2,1)}), bf16[32,34,256]{2,1,0:T(8,128)(2,1)S(1)}, u32[]{:S(2)}, u32[]{:S(2)}) %all-to-all-start) | async-done | bytes 557088 | tf_op jit(solution)/shard_map/all_to_all | solution.py:863
  52.6 1.2 copy.173
  54.5 3.6 constant_dynamic-update-slice_fusion.tok_ref
  58.2 4.0 %pad_maximum_fusion.cot_ref = bf16[2048,1024]{1,0:T(8,128)(2,1)} fusion(bf16[1024,1024]{1,0:T(8,128)(2,1)} %collective-permute-done.1, bf16[1024,1024]{1,0:T(8,128)(2,1)S(1)} %copy-done.9), kind=kLoop, calls=%fused_computation.4 | loop fusion | flops 8388608 | bytes 8388608 | tf_op jit(solution)/shard_map/concatenate | solution.py:850
  62.3 1.3 broadcast_in_dim.52.live_ref
  63.6 9.5 %norm.1 = (bf16[2048,1024]{1,0:T(8,128)(2,1)}, bf16[2048,1024]{1,0:T(8,128)(2,1)}, bf16[256,2048]{1,0:T(8,128)(2,1)}, bf16[256,2048]{1,0:T(8,128)(2,1)}, f32[1,1024]{1,0:T(1,128)S(1)}) custom-call(s32[1]{0:T(128)} %bitcast._.turn_ref, bf16[2048,1024]{1,0:T(8,128)(2,1)} %constant_dynamic-update-slice_fusion.tok_ref, ...), custom_call_target="tpu_custom_call" | custom-call | flops 9900000256 | bytes 33000000 | tf_op jit(solution)/shard_map/norm/pallas_call | solution.py:320
  73.1 3.7 all-to-all-start.1
  77.0 11.4 %mixer_tables.1 = (bf16[32,256,512]{2,1,0:T(8,128)(2,1)}, bf16[32,512,256]{2,1,0:T(8,128)(2,1)}, bf16[32,256,256]{2,1,0:T(8,128)(2,1)}) custom-call(f32[32,1,512]{2,1,0:T(1,128)S(1)} %get-tuple-element.251.lr_ref, f32[32,1,512]{2,1,0:T(1,128)S(1)} %get-tuple-element.250.co_ref), custom_call_target="tpu_custom_call" | custom-call | flops 11879999488 | bytes 39600000 | tf_op jit(solution)/shard_map/mixer_tables/pallas_call | solution.py:256
  88.5 7.5 %all-to-all-done.1.v_ref = bf16[8,32,2048]{2,1,0:T(8,128)(2,1)S(1)} async-done(((bf16[8,32,2048]{2,1,0:T(8,128)(2,1)}), bf16[8,32,2048]{2,1,0:T(8,128)(2,1)S(1)}, u32[]{:S(2)}, u32[]{:S(2)}) %all-to-all-start.1) | async-done | bytes 1048608 | tf_op jit(solution)/shard_map/all_to_all | solution.py:944
  97.0 13.1 %mixer_forward.1 = (bf16[8,32,2048]{2,1,0:T(8,128)(2,1)}, f32[32,64,512]{2,1,0:T(8,128)}) custom-call(s32[1]{0:T(128)} %bitcast._.turn_ref, bf16[8,32,2048]{2,1,0:T(8,128)(2,1)} %copy-done.11, bf16[32,256,512]{2,1,0:T(8,128)(2,1)} %get-tuple-element.81.d_ref, bf16[32,512,256]{2,1,0:T(8,128)(2,1)} %get-tuple-element.82.dt_ref, ...), custom_call_target="tpu_custom_call" | custom-call | flops 12869999616 | bytes 42900000 | tf_op jit(solution)/shard_map/mixer_forward/pallas_call | solution.py:278
  110.1 4.6 %all-to-all-start.2 = ((bf16[8,32,2048]{2,1,0:T(8,128)(2,1)}), bf16[8,32,2048]{2,1,0:T(8,128)(2,1)S(1)}, u32[]{:S(2)}, u32[]{:S(2)}) async-start(bf16[8,32,2048]{2,1,0:T(8,128)(2,1)} %get-tuple-element.84), calls=%async_computation.2 | async-start | bytes 2097152 | tf_op jit(solution)/shard_map/all_to_all | solution.py:944
  114.8 34.0 %all-gather.3.cloned.1.call-done = bf16[15360,512]{1,0:T(8,128)(2,1)} async-done(((bf16[480,512]{1,0:T(8,128)(2,1)}), bf16[15360,512]{1,0:T(8,128)(2,1)}) %all-gather.3.cloned.1.call-update) | async-done | bytes 15728656 | tf_op jit(solution)/shard_map/all_gather | solution.py:892
  148.8 23.8 %early.1 = (bf16[2048,1536]{1,0:T(8,128)(2,1)}, bf16[2048,1536]{1,0:T(8,128)(2,1)}, bf16[2048,1536]{1,0:T(8,128)(2,1)}, f32[256,2048]{1,0:T(8,128)}, bf16[256,20...) custom-call(s32[1]{0:T(128)} %bitcast._.turn_ref, bf16[2048,1024]{1,0:T(8,128)(2,1)} %get-tuple-element.85.x_ref.a_ref.n_ref, ...), custom_call_target="tpu_custom_call" | custom-call | flops 23759998976 | bytes 79200000 | tf_op jit(solution)/shard_map/early/pallas_call | solution.py:320
  173.7 1.8 collective-permute-done.3
  175.4 3.1 add_convert_fusion
  178.6 5.0 %all-to-all-start.3 = ((bf16[8,32,2048]{2,1,0:T(8,128)(2,1)}), bf16[8,32,2048]{2,1,0:T(8,128)(2,1)}, u32[]{:S(2)}, u32[]{:S(2)}) async-start(bf16[8,32,2048]{2,1,0:T(8,128)(2,1)} %bitcast.21), calls=%async_computation.3 | async-start | bytes 2097152 | tf_op jit(solution)/shard_map/all_to_all | solution.py:944
  183.5 11.2 %gate.1 = (bf16[2048,1536]{1,0:T(8,128)(2,1)}, bf16[2048,1536]{1,0:T(8,128)(2,1)}, f32[1,1536]{1,0:T(1,128)S(1)}) custom-call(s32[1]{0:T(128)} %bitcast._.turn_ref, bf16[256,2048]{1,0:T(8,128)(2,1)S(1)} %bitcast.115, bf16[256,2048]{1,0:T(8,128)(2,1)} %collective-permute-done.4.yo_ref, f32[1,1536]{1,0:T(1,128)S(1)} %reshape.505.b3_ref, ...), custom_call_target="tpu_custom_call" | custom-call | flops 12869999616 | bytes 42900000 | tf_op jit(solution)/shard_map/gate/pallas_call | solution.py:320
  195.0 11.1 %grad_four.1 = (f32[384,1024]{1,0:T(8,128)}, bf16[384,1024]{1,0:T(8,128)(2,1)S(1)}, bf16[384,1024]{1,0:T(8,128)(2,1)S(1)}, bf16[384,1024]{1,0:T(8,128)(2,1)}) custom-call(s32[1]{0:T(128)} %bitcast.20.here_ref, bf16[2048,1536]{1,0:T(8,128)(2,1)} %get-tuple-element.92.a_ref.z_ref, bf16[2048,1024]{1,0:T(8,128)(2,1)} %get-tuple-element.86.g_ref.b_ref), custom_call_target="tpu_custom_call" | custom-call | flops 10890000384 | bytes 36300000 | tf_op jit(solution)/shard_map/grad_four/pallas_call | solution.py:320
  206.1 2.0 collective-permute-start.6
  208.1 1.5 collective-permute-start.5
  209.6 19.8 %mixer_backward.1 = (bf16[8,32,2048]{2,1,0:T(8,128)(2,1)}, f32[32,1,512]{2,1,0:T(1,128)S(1)}, f32[32,1,512]{2,1,0:T(1,128)S(1)}, f32[32,1,128]{2,1,0:T(1,128)S(1)}) custom-call(s32[1]{0:T(128)} %bitcast._.turn_ref, bf16[8,32,2048]{2,1,0:T(8,128)(2,1)} %copy-done.11, bf16[8,32,2048]{2,1,0:T(8,128)(2,1)} %all-to-all-done.3.dy_ref, ...), custom_call_target="tpu_custom_call" | custom-call | flops 19800000512 | bytes 66000000 | tf_op jit(solution)/shard_map/mixer_backward/pallas_call | solution.py:278
  229.5 5.1 %all-to-all-start.4 = ((bf16[8,32,2048]{2,1,0:T(8,128)(2,1)}), bf16[8,32,2048]{2,1,0:T(8,128)(2,1)}, u32[]{:S(2)}, u32[]{:S(2)}) async-start(bf16[8,32,2048]{2,1,0:T(8,128)(2,1)} %get-tuple-element.98), calls=%async_computation.4 | async-start | bytes 2097152 | tf_op jit(solution)/shard_map/all_to_all | solution.py:944
  234.6 6.5 %grad_three.1 = (f32[128,1536]{1,0:T(8,128)S(1)}, bf16[128,1536]{1,0:T(8,128)(2,1)S(1)}, bf16[128,1536]{1,0:T(8,128)(2,1)S(1)}, bf16[128,1536]{1,0:T(8,128)(2,1)S(1)}) custom-call(s32[1]{0:T(128)} %bitcast.20.here_ref, bf16[256,2048]{1,0:T(8,128)(2,1)} %bitcast.116, bf16[256,2048]{1,0:T(8,128)(2,1)} %collective-permute-done.4.yo_ref, ...), custom_call_target="tpu_custom_call" | custom-call | flops 7920000000 | bytes 26400000 | tf_op jit(solution)/shard_map/grad_three/pallas_call | solution.py:320
  241.1 11.6 %grad_one.1 = (f32[256,1536]{1,0:T(8,128)}, bf16[256,1536]{1,0:T(8,128)(2,1)S(1)}, bf16[256,1536]{1,0:T(8,128)(2,1)S(1)}, bf16[256,1536]{1,0:T(8,128)(2,1)}) custom-call(s32[1]{0:T(128)} %bitcast.20.here_ref, bf16[2048,1024]{1,0:T(8,128)(2,1)} %get-tuple-element.85.x_ref.a_ref.n_ref, bf16[2048,1536]{1,0:T(8,128)(2,1)} %get-tuple-element.109.b_ref.dh_ref), custom_call_target="tpu_custom_call" | custom-call | flops 11879999488 | bytes 39600000 | tf_op jit(solution)/shard_map/grad_one/pallas_call | solution.py:320
  253.8 1.1 pad_maximum_fusion.3
  254.9 2.9 collective-permute-start.11
  257.9 1.1 pad_maximum_fusion.2
  259.5 1.1 pad_maximum_fusion.1
  260.7 3.1 add_convert_fusion.1
  263.7 12.8 %all-to-all-start.5 = ((bf16[4,96,1024]{2,1,0:T(8,128)(2,1)}), bf16[4,96,1024]{2,1,0:T(8,128)(2,1)S(1)}, u32[]{:S(2)}, u32[]{:S(2)}) async-start(bf16[4,96,1024]{2,1,0:T(8,128)(2,1)} %bitcast.27), calls=%async_computation.5 | async-start | bytes 1572864 | tf_op jit(solution)/shard_map/all_to_all | solution.py:1089
  276.5 20.1 %out.1 = (f32[1024,1024]{1,0:T(8,128)}, bf16[1024,1024]{1,0:T(8,128)(2,1)}, bf16[2048,1024]{1,0:T(8,128)(2,1)}) custom-call(s32[1]{0:T(128)} %bitcast._.turn_ref, bf16[2048,1536]{1,0:T(8,128)(2,1)} %get-tuple-element.92.a_ref.z_ref, bf16[2048,1536]{1,0:T(8,128)(2,1)} %get-tuple-element.109.b_ref.dh_ref, bf16[16,2,480,512]{3,2,1,0:T(8,128)(2,1)} %bitcast.175, ...), custom_call_target="tpu_custom_call" | custom-call | flops 19800000512 | bytes 66000000 | tf_op jit(solution)/shard_map/out/pallas_call | solution.py:320
  296.7 3.0 collective-permute-start.17
  300.7 11.1 %tail.1 = (bf16[1024,256]{1,0:T(8,128)(2,1)S(1)}, f32[1024,1024]{1,0:T(8,128)}, bf16[1024,1024]{1,0:T(8,128)(2,1)}, f32[1,1024]{1,0:T(1,128)S(1)}, f32[1,1024]{1,0:T(1,128)S(1)}, /*index=5*/f32[256,128]{1,0:T(8,128)S(1)}) custom-call(s32[1]{0:T(128)} %bitcast._.turn_ref, bf16[256,2048]{1,0:T(8,128)(2,1)} %bitcast.22.dv_ref, ...), custom_call_target="tpu_custom_call" | custom-call | flops 990000000 | bytes 3300000 | tf_op jit(solution)/shard_map/tail/pallas_call | solution.py:320
  313.3 2.9 fusion.24
  316.3 1.5 collective-permute-start.15
  317.8 1.4 collective-permute-start.14
  319.3 1.4 collective-permute-start.13
  322.3 3.7 all-to-all-start.6
  326.0 5.2 %multiply_convert_fusion = bf16[1024,1024]{1,0:T(8,128)(2,1)} fusion(f32[1024,1024]{1,0:T(8,128)} %get-tuple-element.110, bf16[1024,1024]{1,0:T(8,128)(2,1)} %collective-permute-done.8, bf16[1024,1024]{1,0:T(8,128)(2,1)S(1)} %copy-done.4, f32[1024]{0:T(1024)S(1)} %add.207, f32[1024]{0:T(1024)S(1)} %slice-done), kind=kLoop, calls=%fused_computation.5 | loop fusion | flops 7340032 | bytes 10493952 | tf_op jit(solution)/shard_map/convert_element_type | solution.py:1130
  331.2 7.1 %input_grad.1 = bf16[1024,1024]{1,0:T(8,128)(2,1)} custom-call(s32[1]{0:T(128)} %bitcast._.turn_ref, f32[1024,1024]{1,0:T(8,128)} %get-tuple-element.135.mine_ref, bf16[1024,1024]{1,0:T(8,128)(2,1)} %collective-permute-done.12.got_ref, bf16[1024,1024]{1,0:T(8,128)(2,1)} %tok_ref.1, bf16[2048,1024]{1,0:T(8,128)(2,1)} %get-tuple-element.86.g_ref.b_ref, ...), custom_call_target="tpu_custom_call" | custom-call | flops 6929999872 | bytes 23100000 | tf_op jit(solution)/shard_map/input_grad/pallas_call | solution.py:320
  338.3 15.1 %collective-permute-done.14 = bf16[96,1536]{1,0:T(8,128)(2,1)} collective-permute-done((bf16[96,1536]{1,0:T(8,128)(2,1)}, bf16[96,1536]{1,0:T(8,128)(2,1)}, u32[]{:S(2)}, u32[]{:S(2)}) %collective-permute-start.14) | collective-permute-done | bytes 294944 | tf_op jit(solution)/shard_map/ppermute | solution.py:767
  353.4 1.6 fusion.7
  355.1 4.8 %all-to-all-done.6 = bf16[32,34,256]{2,1,0:T(8,128)(2,1)S(1)} async-done(((bf16[32,34,256]{2,1,0:T(8,128)(2,1)}), bf16[32,34,256]{2,1,0:T(8,128)(2,1)S(1)}, u32[]{:S(2)}, u32[]{:S(2)}) %all-to-all-start.6) | async-done | bytes 557088 | tf_op jit(solution)/shard_map/all_to_all | solution.py:1116
  364.1 1.4 slice.145
  (189 shorter events, 21.6 us)
Async XLA Ops:
  7.2 141.6 %all-gather.3.cloned.1.call-start = ((), (), s32[]{:S(2)}) async-start(), calls=%async_computation.7 | async-start | bytes 16220160 | tf_op jit(solution)/shard_map/all_gather | solution.py:892
  8.5 3.7 %copy-start.3 = (bf16[1024,1024]{1,0:T(8,128)(2,1)S(1)}, bf16[1024,1024]{1,0:T(8,128)(2,1)}, u32[]{:S(2)}) copy-start(bf16[1024,1024]{1,0:T(8,128)(2,1)} %tok_ref.1) | copy-start | bytes 6291460
  8.5 4.3 %copy-start.19 = (bf16[32]{0:T(256)(128)(2,1)S(1)}, bf16[32]{0:T(256)(128)(2,1)}, u32[]{:S(2)}) copy-start(bf16[32]{0:T(256)(128)(2,1)} %param.19) | copy-start | bytes 196
  8.5 4.3 %copy-start.20 = (bf16[32]{0:T(256)(128)(2,1)S(1)}, bf16[32]{0:T(256)(128)(2,1)}, u32[]{:S(2)}) copy-start(bf16[32]{0:T(256)(128)(2,1)} %param.20) | copy-start | bytes 196
  8.5 4.2 %copy-start.21 = (bf16[32]{0:T(256)(128)(2,1)S(1)}, bf16[32]{0:T(256)(128)(2,1)}, u32[]{:S(2)}) copy-start(bf16[32]{0:T(256)(128)(2,1)} %param.28) | copy-start | bytes 196
  8.6 4.2 %copy-start.22 = (bf16[96]{0:T(256)(128)(2,1)S(1)}, bf16[96]{0:T(256)(128)(2,1)}, u32[]{:S(2)}) copy-start(bf16[96]{0:T(256)(128)(2,1)} %param.22) | copy-start | bytes 580
  8.6 4.2 %copy-start.23 = (bf16[96]{0:T(256)(128)(2,1)S(1)}, bf16[96]{0:T(256)(128)(2,1)}, u32[]{:S(2)}) copy-start(bf16[96]{0:T(256)(128)(2,1)} %param.26) | copy-start | bytes 580
  8.6 4.2 %copy-start.24 = (bf16[16]{0:T(256)(128)(2,1)S(1)}, bf16[16]{0:T(256)(128)(2,1)}, u32[]{:S(2)}) copy-start(bf16[16]{0:T(256)(128)(2,1)} %param.24) | copy-start | bytes 100
  8.6 4.5 %copy-start.16 = (bf16[32,512]{1,0:T(8,128)(2,1)S(1)}, bf16[32,512]{1,0:T(8,128)(2,1)}, u32[]{:S(2)}) copy-start(bf16[32,512]{1,0:T(8,128)(2,1)} %param.23) | copy-start | bytes 98308
  12.2 9.4 %copy-start.17 = (f32[16]{0:T(128)S(1)}, f32[16]{0:T(128)}, u32[]{:S(2)}) copy-start(f32[16]{0:T(128)} %param.31) | copy-start | bytes 196
  12.2 9.5 %copy-start.13 = (f32[16,512]{1,0:T(8,128)S(1)}, f32[16,512]{1,0:T(8,128)}, u32[]{:S(2)}) copy-start(f32[16,512]{1,0:T(8,128)} %param.30) | copy-start | bytes 98308
  12.2 9.5 %copy-start.14 = (f32[16,512]{1,0:T(8,128)S(1)}, f32[16,512]{1,0:T(8,128)}, u32[]{:S(2)}) copy-start(f32[16,512]{1,0:T(8,128)} %param.29) | copy-start | bytes 98308
  12.2 12.2 %copy-start.18 = (s32[2]{0:T(128)S(1)}, s32[2]{0:T(128)}, u32[]{:S(2)}) copy-start(s32[2]{0:T(128)} %param.18) | copy-start | bytes 28
  12.3 42.2 %collective-permute-start = (bf16[1024,1024]{1,0:T(8,128)(2,1)S(1)}, bf16[1024,1024]{1,0:T(8,128)(2,1)}, u32[]{:S(2)}, u32[]{:S(2)}) collective-permute-start(bf16[1024,1024]{1,0:T(8,128)(2,1)S(1)} %copy-done.3), channel_id=1, source_target_pairs={{0,1},{1,0},{2,3},{3,2},{4,5},{5,4},{6,7},{7,6},{8,9},{9,8},{10,11... | collective-permute-start | bytes 6291464 | tf_op jit(solution)/shard_map/ppermute | solution.py:763
  14.4 37.4 %all-to-all-start = ((bf16[32,34,256]{2,1,0:T(8,128)(2,1)}), bf16[32,34,256]{2,1,0:T(8,128)(2,1)S(1)}, u32[]{:S(2)}, u32[]{:S(2)}) async-start(bf16[32,34,256]{2,1,0:T(8,128)(2,1)} %bitcast.4), calls=%async_computation | async-start | bytes 1310720 | tf_op jit(solution)/shard_map/all_to_all | solution.py:863
  21.4 36.8 %collective-permute-start.1 = (bf16[1024,1024]{1,0:T(8,128)(2,1)}, bf16[1024,1024]{1,0:T(8,128)(2,1)}, u32[]{:S(2)}, u32[]{:S(2)}) collective-permute-start(bf16[1024,1024]{1,0:T(8,128)(2,1)} %param.17), channel_id=1, source_target_pairs={{0,1},{1,0},{2,3},{3,2},{4,5},{5,4},{6,7},{7,6},{8,9},{9,8},{10,11... | collective-permute-start | bytes 6291464 | tf_op jit(solution)/shard_map/ppermute | solution.py:763
  21.8 55.0 %collective-permute-start.2 = (f32[16,1152]{1,0:T(8,128)S(1)}, f32[16,1152]{1,0:T(8,128)S(1)}, u32[]{:S(2)}, u32[]{:S(2)}) collective-permute-start(f32[16,1152]{1,0:T(8,128)S(1)} %pad_maximum_fusion.12), channel_id=1, source_target_pairs={{0,16},{2,18},{4,20},{6,22},{8,24},{10,26},{12,28},{14,30},{16,0},... | collective-permute-start | bytes 221192 | tf_op jit(solution)/shard_map/ppermute | solution.py:767
  26.0 147.1 %copy-start.15 = (f32[2048]{0:T(1024)}, f32[2048]{0:T(1024)S(1)}, u32[]{:S(2)}) copy-start(f32[2048]{0:T(1024)S(1)} %fusion.32) | copy-start | bytes 24580
  54.3 9.3 %copy-start.1 = (f32[1,1024]{1,0:T(1,128)}, f32[1,1024]{1,0:T(1,128)S(1)}, u32[]{:S(2)}) copy-start(f32[1,1024]{1,0:T(1,128)S(1)} %reshape.491.gain_ref) | copy-start | bytes 12292
  73.1 23.0 %all-to-all-start.1 = ((bf16[8,32,2048]{2,1,0:T(8,128)(2,1)}), bf16[8,32,2048]{2,1,0:T(8,128)(2,1)S(1)}, u32[]{:S(2)}, u32[]{:S(2)}) async-start(bf16[8,32,2048]{2,1,0:T(8,128)(2,1)} %bitcast.9), calls=%async_computation.1 | async-start | bytes 2097152 | tf_op jit(solution)/shard_map/all_to_all | solution.py:944
  110.1 62.8 %all-to-all-start.2 = ((bf16[8,32,2048]{2,1,0:T(8,128)(2,1)}), bf16[8,32,2048]{2,1,0:T(8,128)(2,1)S(1)}, u32[]{:S(2)}, u32[]{:S(2)}) async-start(bf16[8,32,2048]{2,1,0:T(8,128)(2,1)} %get-tuple-element.84), calls=%async_computation.2 | async-start | bytes 2097152 | tf_op jit(solution)/shard_map/all_to_all | solution.py:944
  172.6 2.8 collective-permute-start.3
  172.9 10.6 %copy-start = (bf16[8,32,2048]{2,1,0:T(8,128)(2,1)}, bf16[8,32,2048]{2,1,0:T(8,128)(2,1)S(1)}, u32[]{:S(2)}) copy-start(bf16[8,32,2048]{2,1,0:T(8,128)(2,1)S(1)} %all-to-all-done.2) | copy-start | bytes 3145732
  172.9 10.6 %collective-permute-start.4 = (bf16[256,2048]{1,0:T(8,128)(2,1)S(1)}, bf16[256,2048]{1,0:T(8,128)(2,1)}, u32[]{:S(2)}, u32[]{:S(2)}) collective-permute-start(bf16[256,2048]{1,0:T(8,128)(2,1)S(1)} %bitcast.114), channel_id=1, source_target_pairs={{0,1},{1,0},{2,3},{3,2},{4,5},{5,4},{6,7},{7,6},{8,9},{9,8},{10,11... | collective-permute-start | bytes 3145736 | tf_op jit(solution)/shard_map/ppermute | solution.py:763
  178.6 31.1 %all-to-all-start.3 = ((bf16[8,32,2048]{2,1,0:T(8,128)(2,1)}), bf16[8,32,2048]{2,1,0:T(8,128)(2,1)}, u32[]{:S(2)}, u32[]{:S(2)}) async-start(bf16[8,32,2048]{2,1,0:T(8,128)(2,1)} %bitcast.21), calls=%async_computation.3 | async-start | bytes 2097152 | tf_op jit(solution)/shard_map/all_to_all | solution.py:944
  206.1 46.7 %collective-permute-start.6 = (bf16[2,2,96,1024]{3,2,1,0:T(8,128)(2,1)S(1)}, bf16[2,2,96,1024]{3,2,1,0:T(8,128)(2,1)}, u32[]{:S(2)}, u32[]{:S(2)}) collective-permute-start(bf16[2,2,96,1024]{3,2,1,0:T(8,128)(2,1)S(1)} %bitcast.126), channel_id=1, source_target_pairs={{0,4},{2,6},{4,0},{6,2},{8,12},{10,14},{12,8},{14,10},{16,20},{18,... | collective-permute-start | bytes 2359304 | tf_op jit(solution)/shard_map/ppermute | solution.py:767
  208.1 44.8 %collective-permute-start.5 = (bf16[2,2,96,1024]{3,2,1,0:T(8,128)(2,1)S(1)}, bf16[2,2,96,1024]{3,2,1,0:T(8,128)(2,1)}, u32[]{:S(2)}, u32[]{:S(2)}) collective-permute-start(bf16[2,2,96,1024]{3,2,1,0:T(8,128)(2,1)S(1)} %bitcast.125), channel_id=1, source_target_pairs={{0,2},{2,0},{4,6},{6,4},{8,10},{10,8},{12,14},{14,12},{16,18},{18,... | collective-permute-start | bytes 2359304 | tf_op jit(solution)/shard_map/ppermute | solution.py:767
  209.6 43.3 %collective-permute-start.7 = (bf16[2,2,96,1024]{3,2,1,0:T(8,128)(2,1)}, bf16[2,2,96,1024]{3,2,1,0:T(8,128)(2,1)}, u32[]{:S(2)}, u32[]{:S(2)}) collective-permute-start(bf16[2,2,96,1024]{3,2,1,0:T(8,128)(2,1)} %bitcast.177), channel_id=1, source_target_pairs={{0,6},{2,4},{4,2},{6,0},{8,14},{10,12},{12,10},{14,8},{16,22},{18,... | collective-permute-start | bytes 2359304 | tf_op jit(solution)/shard_map/ppermute | solution.py:767
  229.5 34.3 %all-to-all-start.4 = ((bf16[8,32,2048]{2,1,0:T(8,128)(2,1)}), bf16[8,32,2048]{2,1,0:T(8,128)(2,1)}, u32[]{:S(2)}, u32[]{:S(2)}) async-start(bf16[8,32,2048]{2,1,0:T(8,128)(2,1)} %get-tuple-element.98), calls=%async_computation.4 | async-start | bytes 2097152 | tf_op jit(solution)/shard_map/all_to_all | solution.py:944
  254.9 58.4 %collective-permute-start.11 = (bf16[2,2,96,1536]{3,2,1,0:T(8,128)(2,1)}, bf16[2,2,96,1536]{3,2,1,0:T(8,128)(2,1)}, u32[]{:S(2)}, u32[]{:S(2)}) collective-permute-start(bf16[2,2,96,1536]{3,2,1,0:T(8,128)(2,1)} %pad_maximum_fusion.3), channel_id=1, source_target_pairs={{0,6},{2,4},{4,2},{6,0},{8,14},{10,12},{12,10},{14,8},{16,22},{18,... | collective-permute-start | bytes 3538952 | tf_op jit(solution)/shard_map/ppermute | solution.py:767
  259.0 54.3 %collective-permute-start.10 = (bf16[2,2,96,1536]{3,2,1,0:T(8,128)(2,1)}, bf16[2,2,96,1536]{3,2,1,0:T(8,128)(2,1)}, u32[]{:S(2)}, u32[]{:S(2)}) collective-permute-start(bf16[2,2,96,1536]{3,2,1,0:T(8,128)(2,1)} %pad_maximum_fusion.2), channel_id=1, source_target_pairs={{0,4},{2,6},{4,0},{6,2},{8,12},{10,14},{12,8},{14,10},{16,20},{18,... | collective-permute-start | bytes 3538952 | tf_op jit(solution)/shard_map/ppermute | solution.py:767
  260.6 52.7 %collective-permute-start.9 = (bf16[2,2,96,1536]{3,2,1,0:T(8,128)(2,1)}, bf16[2,2,96,1536]{3,2,1,0:T(8,128)(2,1)}, u32[]{:S(2)}, u32[]{:S(2)}) collective-permute-start(bf16[2,2,96,1536]{3,2,1,0:T(8,128)(2,1)} %pad_maximum_fusion.1), channel_id=1, source_target_pairs={{0,2},{2,0},{4,6},{6,4},{8,10},{10,8},{12,14},{14,12},{16,18},{18,... | collective-permute-start | bytes 3538952 | tf_op jit(solution)/shard_map/ppermute | solution.py:767
  263.7 36.0 %all-to-all-start.5 = ((bf16[4,96,1024]{2,1,0:T(8,128)(2,1)}), bf16[4,96,1024]{2,1,0:T(8,128)(2,1)S(1)}, u32[]{:S(2)}, u32[]{:S(2)}) async-start(bf16[4,96,1024]{2,1,0:T(8,128)(2,1)} %bitcast.27), calls=%async_computation.5 | async-start | bytes 1572864 | tf_op jit(solution)/shard_map/all_to_all | solution.py:1089
  296.6 29.4 %collective-permute-start.8 = (bf16[1024,1024]{1,0:T(8,128)(2,1)}, bf16[1024,1024]{1,0:T(8,128)(2,1)}, u32[]{:S(2)}, u32[]{:S(2)}) collective-permute-start(bf16[1024,1024]{1,0:T(8,128)(2,1)} %get-tuple-element.111), channel_id=1, source_target_pairs={{0,1},{1,0},{2,3},{3,2},{4,5},{5,4},{6,7},{7,6},{8,9},{9,8},{10,11... | collective-permute-start | bytes 6291464 | tf_op jit(solution)/shard_map/ppermute | solution.py:763
  296.7 15.1 %collective-permute-start.17 = (f32[16,1152]{1,0:T(8,128)S(1)}, f32[16,1152]{1,0:T(8,128)S(1)}, u32[]{:S(2)}, u32[]{:S(2)}) collective-permute-start(f32[16,1152]{1,0:T(8,128)S(1)} %dynamic-slice_bitcast_fusion), channel_id=1, source_target_pairs={{0,16},{2,18},{4,20},{6,22},{8,24},{10,26},{12,28},{14,30},{16,0},... | collective-permute-start | bytes 221192 | tf_op jit(solution)/shard_map/ppermute | solution.py:767
  299.7 13.6 %copy-start.5 = (f32[2,2,2,16,1536]{4,3,2,1,0:T(8,128)}, f32[2,2,2,16,1536]{4,3,2,1,0:T(8,128)S(1)}, u32[]{:S(2)}) copy-start(f32[2,2,2,16,1536]{4,3,2,1,0:T(8,128)S(1)} %copy.179) | copy-start | bytes 2359300
  300.7 12.6 %copy-start.7 = (f32[256,1536]{1,0:T(8,128)S(1)}, f32[256,1536]{1,0:T(8,128)}, u32[]{:S(2)}) copy-start(f32[256,1536]{1,0:T(8,128)} %get-tuple-element.102) | copy-start | bytes 4718596
  311.8 19.4 %collective-permute-start.12 = (bf16[1024,1024]{1,0:T(8,128)(2,1)}, bf16[1024,1024]{1,0:T(8,128)(2,1)}, u32[]{:S(2)}, u32[]{:S(2)}) collective-permute-start(bf16[1024,1024]{1,0:T(8,128)(2,1)} %get-tuple-element.136), channel_id=1, source_target_pairs={{0,1},{1,0},{2,3},{3,2},{4,5},{5,4},{6,7},{7,6},{8,9},{9,8},{10,11... | collective-permute-start | bytes 6291464 | tf_op jit(solution)/shard_map/ppermute | solution.py:763
  316.3 9.7 %copy-start.4 = (bf16[1024,1024]{1,0:T(8,128)(2,1)S(1)}, bf16[1024,1024]{1,0:T(8,128)(2,1)}, u32[]{:S(2)}) copy-start(bf16[1024,1024]{1,0:T(8,128)(2,1)} %tok_ref.1) | copy-start | bytes 6291460
  316.3 9.7 %slice-start = ((f32[2048]{0:T(1024)}), f32[1024]{0:T(1024)S(1)}, s32[]{:S(2)}) async-start(f32[2048]{0:T(1024)} %copy-done.15), calls=%async_computation.8 | async-start | bytes 8192 | tf_op jit(solution)/shard_map/slice | solution.py:1130
  316.3 22.0 %collective-permute-start.15 = (bf16[96,1536]{1,0:T(8,128)(2,1)}, bf16[96,1536]{1,0:T(8,128)(2,1)}, u32[]{:S(2)}, u32[]{:S(2)}) collective-permute-start(bf16[96,1536]{1,0:T(8,128)(2,1)} %get-tuple-element.239), channel_id=1, source_target_pairs={{0,24},{2,26},{4,28},{6,30},{8,16},{10,18},{12,20},{14,22},{16,8},... | collective-permute-start | bytes 884744 | tf_op jit(solution)/shard_map/ppermute | solution.py:767
  317.8 35.5 %collective-permute-start.14 = (bf16[96,1536]{1,0:T(8,128)(2,1)}, bf16[96,1536]{1,0:T(8,128)(2,1)}, u32[]{:S(2)}, u32[]{:S(2)}) collective-permute-start(bf16[96,1536]{1,0:T(8,128)(2,1)} %get-tuple-element.240), channel_id=1, source_target_pairs={{0,16},{2,18},{4,20},{6,22},{8,24},{10,26},{12,28},{14,30},{16,0},... | collective-permute-start | bytes 884744 | tf_op jit(solution)/shard_map/ppermute | solution.py:767
  319.3 34.1 %collective-permute-start.13 = (bf16[96,1536]{1,0:T(8,128)(2,1)}, bf16[96,1536]{1,0:T(8,128)(2,1)}, u32[]{:S(2)}, u32[]{:S(2)}) collective-permute-start(bf16[96,1536]{1,0:T(8,128)(2,1)} %get-tuple-element.241), channel_id=1, source_target_pairs={{0,8},{2,10},{4,12},{6,14},{8,0},{10,2},{12,4},{14,6},{16,24},{18,... | collective-permute-start | bytes 884744 | tf_op jit(solution)/shard_map/ppermute | solution.py:767
  322.3 37.6 %all-to-all-start.6 = ((bf16[32,34,256]{2,1,0:T(8,128)(2,1)}), bf16[32,34,256]{2,1,0:T(8,128)(2,1)S(1)}, u32[]{:S(2)}, u32[]{:S(2)}) async-start(bf16[32,34,256]{2,1,0:T(8,128)(2,1)} %pad_maximum_fusion.4), calls=%async_computation.6 | async-start | bytes 1310720 | tf_op jit(solution)/shard_map/all_to_all | solution.py:1116
  326.0 5.2 %copy-start.2 = (f32[1,1024]{1,0:T(1,128)S(1)}, f32[1,1024]{1,0:T(1,128)}, u32[]{:S(2)}) copy-start(f32[1,1024]{1,0:T(1,128)} %copy-done.1) | copy-start | bytes 12292
  331.2 22.2 %copy-start.6 = (f32[2,2,2,16,1536]{4,3,2,1,0:T(8,128)S(1)}, f32[2,2,2,16,1536]{4,3,2,1,0:T(8,128)}, u32[]{:S(2)}) copy-start(f32[2,2,2,16,1536]{4,3,2,1,0:T(8,128)} %copy-done.5) | copy-start | bytes 2359300
  331.2 22.2 %copy-start.8 = (f32[256,1536]{1,0:T(8,128)S(1)}, f32[256,1536]{1,0:T(8,128)}, u32[]{:S(2)}) copy-start(f32[256,1536]{1,0:T(8,128)} %get-tuple-element.102) | copy-start | bytes 4718596
  360.0 2.8 collective-permute-start.16
  (4 other events, 8.6 us)
Sparse Core Ops, SparseCore 0:
  12.4 136.3 all-gather.2
